TPU v7x, 128 devices: a whole 4x4x4 slice. The times are simulated.
128 devices in a mesh: dp: 8 (over y, core), seq: 16 (over z, x).
Axes of the slice: x: 4, y: 4, z: 4, core: 2. Of those that a mesh axis runs over, the one named last changes fastest.
Arguments:
- x_branch: bfloat16 [8, 2048, 8192], P('dp', 'seq'), may hold values from -6 to 6
- z_branch: bfloat16 [8, 2048, 8192], P('dp', 'seq'), may hold values from -6 to 6
- out_grad: bfloat16 [8, 2048, 8192], P('dp', 'seq'), may hold values from -6 to 6
- x_weight: bfloat16 [8192, 288], P('seq', 'dp'), may hold values from -0.0625 to 0.0625
- dt_weight: bfloat16 [256, 8192], P('dp', 'seq'), may hold values from -0.375 to 0.375
- conv_weight: float32 [4, 8192], replicated, may hold values from -3 to 3
- conv_bias: float32 [8192], replicated, may hold values from -0.5 to 0.5
- dt_bias: float32 [8192], replicated, may hold values from -4.5 to -3.5
- a_log: float32 [16, 8192], replicated, may hold values from -12 to 1
- d_skip: float32 [8192], replicated, may hold values from 0.5 to 1.5
Outputs:
- mixer_out: bfloat16 [8, 2048, 8192], P('dp', 'seq')
- grad_x_branch: bfloat16 [8, 2048, 8192], P('dp', 'seq')
- grad_z_branch: bfloat16 [8, 2048, 8192], P('dp', 'seq')
- grad_x_weight: float32 [8192, 288], P('seq', 'dp')
- grad_dt_weight: float32 [256, 8192], P('dp', 'seq')
- grad_conv_weight: float32 [4, 8192], replicated
- grad_conv_bias: float32 [8192], replicated
- grad_dt_bias: float32 [8192], replicated
- grad_a_log: float32 [16, 8192], replicated
- grad_d_skip: float32 [8192], replicated
All inputs are finite; a program needn't handle non-finite values.
Results may differ from a plain program's by a relative error of at most 0.007.
Values may be sent and summed in bfloat16 or wider, within the bound.
A program may use at most 256 MiB of HBM per device.

v0:
```python
import jax
import jax.numpy as jnp
from jax import lax
from jax.sharding import PartitionSpec as P

N = 16
R = 256


def from_behind(value, axis, steps):
    count = lax.axis_size(axis)
    leading, last = (max(0, -steps), min(count, count - steps))
    return lax.ppermute(value, axis, [(source, source + steps) for source in range(leading, last)])


def carried_in(value, axis, join, neutral, backward):
    count, mine = (lax.axis_size(axis), lax.axis_index(axis))
    pieces = jax.tree.map(lambda part: lax.all_gather(part, axis), value)
    if backward:
        pieces = jax.tree.map(lambda part: part[::-1], pieces)
        mine = count - 1 - mine
    so_far = jax.tree.map(
        lambda part, zero: jnp.full_like(part, 0) + jnp.asarray(zero, part.dtype), value, neutral
    )

    def hop(position, so_far):
        longer = join(so_far, jax.tree.map(lambda part: part[position], pieces))
        return jax.tree.map(lambda new, old: jnp.where(position < mine, new, old), longer, so_far)

    return lax.fori_loop(0, count - 1, hop, so_far)


def silu_slope(values):
    logistic = jax.nn.sigmoid(values)
    return logistic * (1.0 + values * (1.0 - logistic))


def chain_combine(earlier, later):
    return (earlier[0] * later[0], later[0] * earlier[1] + later[1])


def weighted_sum(a_mat, exponents, left_rows, right_rows, block_len):
    block_count = exponents.shape[0] // block_len

    def shaped(source):
        return source.reshape((block_count, block_len) + source.shape[1:])

    def accumulate(running, pieces):
        exponent_part, left_part, right_part = pieces
        term_block = (
            jnp.exp(exponent_part[:, None, :] * a_mat[None])
            * left_part[:, :, None]
            * right_part[:, None, :]
        )
        return (running + jnp.sum(term_block, axis=0), None)

    result, unused = lax.scan(
        accumulate,
        jnp.zeros(a_mat.shape, jnp.float32),
        (shaped(exponents), shaped(left_rows), shaped(right_rows)),
    )
    return result


def forward_pass(a_mat, start_state, step_size, drive_term, b_mat, c_mat, block_len):
    block_count = step_size.shape[0] // block_len

    def shaped(source):
        return source.reshape((block_count, block_len) + source.shape[1:])

    def advance(carried, pieces):
        step_blk, drive_blk, b_blk, c_blk = pieces
        first_state = carried
        outputs = []
        for offset in range(block_len):
            carried = (
                jnp.exp(step_blk[offset][None, :] * a_mat) * carried
                + b_blk[offset][:, None] * drive_blk[offset][None, :]
            )
            outputs.append(jnp.sum(c_blk[offset][:, None] * carried, axis=0))
        return (carried, (first_state, jnp.stack(outputs)))

    final_state, (checks, scanned) = lax.scan(
        advance, start_state, (shaped(step_size), shaped(drive_term), shaped(b_mat), shaped(c_mat))
    )
    return (checks, scanned.reshape(step_size.shape))


def backward_pass(a_mat, checks, entering, step_size, drive_term, b_mat, c_mat, g_state, block_len):
    block_count = step_size.shape[0] // block_len

    def shaped(source):
        return source.reshape((block_count, block_len) + source.shape[1:])

    def retreat(carried, pieces):
        adjoint_next, rate_grad = carried
        first_state, step_blk, drive_blk, b_blk, c_blk, g_blk = pieces
        history = []
        current = first_state
        for offset in range(block_len):
            factor = jnp.exp(step_blk[offset][None, :] * a_mat)
            updated = factor * current + b_blk[offset][:, None] * drive_blk[offset][None, :]
            history.append((factor, current, updated))
            current = updated
        drive_grads, rate_grads, b_grads, c_grads = ([], [], [], [])
        for offset in range(block_len - 1, -1, -1):
            factor, earlier, updated = history[offset]
            adjoint = c_blk[offset][:, None] * g_blk[offset][None, :] + adjoint_next
            drive_grads.append(jnp.sum(adjoint * b_blk[offset][:, None], axis=0))
            b_grads.append(jnp.sum(adjoint * drive_blk[offset][None, :], axis=1))
            c_grads.append(jnp.sum(updated * g_blk[offset][None, :], axis=1))
            moment = adjoint * factor * earlier
            rate_grads.append(jnp.sum(moment * a_mat, axis=0))
            rate_grad = rate_grad + moment * step_blk[offset][None, :]
            adjoint_next = factor * adjoint
        stacked = tuple(
            (
                jnp.stack(collected[::-1])
                for collected in (drive_grads, rate_grads, b_grads, c_grads)
            )
        )
        return ((adjoint_next, rate_grad), stacked)

    pieces_all = (
        checks,
        shaped(step_size),
        shaped(drive_term),
        shaped(b_mat),
        shaped(c_mat),
        shaped(g_state),
    )
    carried, stacked = lax.scan(
        retreat, (entering, jnp.zeros(a_mat.shape, jnp.float32)), pieces_all, reverse=True
    )
    flattened = tuple(
        (
            stacked_part.reshape((step_size.shape[0],) + stacked_part.shape[2:])
            for stacked_part in stacked
        )
    )
    return (carried[1], flattened)


def local(
    x_branch,
    z_branch,
    out_grad,
    x_weight,
    dt_weight,
    conv_weight,
    conv_bias,
    dt_bias,
    a_log,
    d_skip,
):
    x_tok = x_branch[0]
    z_tok = z_branch[0]
    g_tok = out_grad[0]
    tok_count = x_tok.shape[0]
    tap_count = conv_weight.shape[0]
    x_panel, dt_panel = (
        lax.all_gather(x_weight, "dp", axis=1, tiled=True),
        lax.all_gather(dt_weight, "dp", axis=0, tiled=True),
    )
    previous = from_behind(x_tok[tok_count - tap_count + 1 :], "seq", 1)
    extended = jnp.concatenate([previous, x_tok], axis=0).astype(jnp.float32)
    conv_pre = jnp.zeros(x_tok.shape, jnp.float32) + conv_bias[None, :]
    for tap_index in range(tap_count):
        conv_pre = (
            conv_pre + conv_weight[tap_index][None, :] * extended[tap_index : tap_index + tok_count]
        )
    x_conv = jax.nn.silu(conv_pre).astype(jnp.bfloat16)
    x_full, dt_full = (
        lax.all_gather(x_panel, "seq", axis=0, tiled=True),
        lax.all_gather(dt_panel, "seq", axis=1, tiled=True),
    )
    projected = jnp.dot(x_conv, x_full, preferred_element_type=jnp.float32)
    low_part = projected[:, :R].astype(jnp.bfloat16)
    rate_lin = jnp.dot(low_part, dt_full, preferred_element_type=jnp.float32)
    b_mat = projected[:, R : R + N]
    c_mat = projected[:, R + N :]
    rate_pre = rate_lin + dt_bias[None, :]
    step_size = jax.nn.softplus(rate_pre)
    a_mat = -jnp.exp(a_log)
    x_wide = x_conv.astype(jnp.float32)
    drive_term = step_size * x_wide
    block_len = max(8, tok_count // 16)
    cumul = jnp.cumsum(step_size, axis=0)
    total_rate = cumul[tok_count - 1]
    decay_all = jnp.exp(a_mat * total_rate[None, :])
    local_end = weighted_sum(a_mat, total_rate[None, :] - cumul, b_mat, drive_term, block_len)
    identity = (jnp.ones(a_mat.shape, jnp.float32), jnp.zeros(a_mat.shape, jnp.float32))
    entering = carried_in((decay_all, local_end), "seq", chain_combine, identity, False)
    checks, scanned = forward_pass(
        a_mat, entering[1], step_size, drive_term, b_mat, c_mat, block_len
    )
    z_wide = z_tok.astype(jnp.float32)
    gate_act = jax.nn.silu(z_wide)
    inner_sum = scanned + d_skip[None, :] * x_wide
    mixer_out = (gate_act * inner_sum).astype(jnp.bfloat16)
    g_wide = g_tok.astype(jnp.float32)
    g_state = g_wide * gate_act
    grad_z = (g_wide * inner_sum * silu_slope(z_wide)).astype(jnp.bfloat16)
    adjoint_local = weighted_sum(a_mat, cumul, c_mat, g_state, block_len)
    leaving = carried_in((decay_all, adjoint_local), "seq", chain_combine, identity, True)
    g_amat, (g_drive, g_rate, g_bmat, g_cmat) = backward_pass(
        a_mat, checks, leaving[1], step_size, drive_term, b_mat, c_mat, g_state, block_len
    )
    g_pre = (g_drive * x_wide + g_rate) * jax.nn.sigmoid(rate_pre)
    g_pre_b = g_pre.astype(jnp.bfloat16)
    g_wdt_full = jnp.dot(low_part.T, g_pre_b, preferred_element_type=jnp.float32)
    g_low = jnp.dot(g_pre_b, dt_full.T, preferred_element_type=jnp.float32)
    g_proj = jnp.concatenate([g_low, g_bmat, g_cmat], axis=1).astype(jnp.bfloat16)
    g_wx_full = jnp.dot(x_conv.T, g_proj, preferred_element_type=jnp.float32)
    g_matmul = jnp.dot(g_proj, x_full.T, preferred_element_type=jnp.float32)
    g_wx_seq, g_wdt_seq = (
        lax.psum_scatter(g_wx_full, "seq", scatter_dimension=0, tiled=True),
        lax.psum_scatter(g_wdt_full, "seq", scatter_dimension=1, tiled=True),
    )
    g_wx_out, g_wdt_out = (
        lax.psum_scatter(g_wx_seq, "dp", scatter_dimension=1, tiled=True),
        lax.psum_scatter(g_wdt_seq, "dp", scatter_dimension=0, tiled=True),
    )
    g_conv_x = g_drive * step_size + g_state * d_skip[None, :] + g_matmul
    g_conv = g_conv_x * silu_slope(conv_pre)
    following = from_behind(g_conv[: tap_count - 1], "seq", -1)
    g_extended = jnp.concatenate([g_conv, following], axis=0)
    grad_x = jnp.zeros(x_tok.shape, jnp.float32)
    for tap_index in range(tap_count):
        begin = tap_count - 1 - tap_index
        grad_x = grad_x + conv_weight[tap_index][None, :] * g_extended[begin : begin + tok_count]
    grad_conv_w = jnp.stack(
        [
            jnp.sum(g_conv * extended[tap_index : tap_index + tok_count], axis=0)
            for tap_index in range(tap_count)
        ]
    )
    grad_conv_b = jnp.sum(g_conv, axis=0)
    grad_bias = jnp.sum(g_pre, axis=0)
    grad_alog = g_amat * a_mat
    grad_skip = jnp.sum(g_state * x_wide, axis=0)
    summed = lax.psum((grad_conv_w, grad_conv_b, grad_bias, grad_alog, grad_skip), ("dp", "seq"))
    return (
        mixer_out[None],
        grad_x.astype(jnp.bfloat16)[None],
        grad_z[None],
        g_wx_out,
        g_wdt_out,
        summed[0],
        summed[1],
        summed[2],
        summed[3],
        summed[4],
    )


def solution(mesh):
    in_specs = (
        P("dp", "seq", None),
        P("dp", "seq", None),
        P("dp", "seq", None),
        P("seq", "dp"),
        P("dp", "seq"),
        P(),
        P(),
        P(),
        P(),
        P(),
    )
    out_specs = (
        P("dp", "seq", None),
        P("dp", "seq", None),
        P("dp", "seq", None),
        P("seq", "dp"),
        P("dp", "seq"),
        P(),
        P(),
        P(),
        P(),
        P(),
    )
    return jax.shard_map(local, mesh=mesh, in_specs=in_specs, out_specs=out_specs, check_vma=False)
```

profile of v0, /device:TPU:1, one launch (start us, length us, event | category | flops | bytes accessed | tf_op | source)
XLA Modules:
  0.0 1775.6 jit_solution(12904991972283140153)
XLA Ops:
  7.2 15.0 all-gather.3
  23.0 14.1 all_gather.34
  41.5 5.4 fusion.38
  49.7 7.6 fusion.50
  57.4 26.8 %all-gather.10.cloned.1.call-done = bf16[8192,288]{0,1:T(8,128)(2,1)} async-done(((bf16[512,288]{0,1:T(8,128)(2,1)}), bf16[8192,288]{0,1:T(8,128)(2,1)}) %all-gather.10.cloned.1.call-update) | async-done | bytes 4718608 | tf_op jit(solution)/shard_map/all_gather | solution.py:174
  87.9 55.4 %all-gather.12.cloned.1.call-done = bf16[256,8192]{1,0:T(8,128)(2,1)} async-done(((bf16[256,512]{1,0:T(8,128)(2,1)}), bf16[256,8192]{1,0:T(8,128)(2,1)}) %all-gather.12.cloned.1.call-update) | async-done | bytes 4194320 | tf_op jit(solution)/shard_map/all_gather | solution.py:175
  146.2 6.7 fusion.63
  152.9 144.3 %reduce_window_sum.13 = f32[128,8192]{1,0:T(8,128)} reduce-window(f32[128,8192]{1,0:T(8,128)} %get-tuple-element.1020, f32[]{:T(128)} %constant.155.clone.1), window={size=128x1 pad=127_0x0_0}, to_apply=%region_0.1 | reduce-window | flops 133169152 | bytes 8388612 | tf_op jit(solution)/shard_map/jit(cumsum)/reduce_window_sum | solution.py:188
  299.9 44.7 %while.92 = (s32[]{:T(128)}, f32[16,8192]{1,0:T(8,128)S(1)}, f32[16,8,8192]{2,1,0:T(8,128)}, f32[16,8192]{1,0:T(8,128)S(1)}, f32[16,8,16]{2,1,0:T(8,128)}, /*index=5*/f32[16,8,8192]{2,1,0:T(8,128)}, s32[]{:T(128)}, s32[]{:T(128)}) while((s32[]{:T(128)}, f32[16,8192]{1,0:T(8,128)S(1)}, f32[16,8,8192]{2,1,0:T(8,128)}, ...), condition=%wide.region_18.19_spmd.clone, body=%wide.region_16.18_spmd.clone.sunk | while | flops 4325379 | bytes 4195943 | solution.py:57
  346.3 4.5 broadcast_subtract_fusion
  350.9 45.3 %while.90 = (s32[]{:T(128)}, f32[16,8192]{1,0:T(8,128)S(1)}, f32[16,8,8192]{2,1,0:T(8,128)}, f32[16,8192]{1,0:T(8,128)S(1)}, f32[16,8,16]{2,1,0:T(8,128)}, /*index=5*/f32[16,8,8192]{2,1,0:T(8,128)}, s32[]{:T(128)}, s32[]{:T(128)}) while((s32[]{:T(128)}, f32[16,8192]{1,0:T(8,128)S(1)}, f32[16,8,8192]{2,1,0:T(8,128)}, ...), condition=%wide.region_3.4_spmd.clone, body=%wide.region_1.3_spmd.clone.sunk | while | flops 4325379 | bytes 4195943 | solution.py:57
  397.1 19.6 %all-gather.18.cloned.1.call-done = f32[256,8192]{1,0:T(8,128)} async-done(((f32[16,8192]{1,0:T(8,128)}), f32[256,8192]{1,0:T(8,128)}) %all-gather.18.cloned.1.call-update) | async-done | bytes 8388624 | tf_op jit(solution)/shard_map/all_gather | solution.py:18
  416.6 7.5 rev.7
  424.1 65.6 %all-gather.14.cloned.1.call-done = f32[256,8192]{1,0:T(8,128)} async-done(((f32[16,8192]{1,0:T(8,128)}), f32[256,8192]{1,0:T(8,128)}) %all-gather.14.cloned.1.call-update) | async-done | bytes 8388624 | tf_op jit(solution)/shard_map/all_gather | solution.py:18
  489.7 7.5 rev.6
  497.2 25.3 %while.93 = (s32[]{:T(128)}, f32[16,8192]{1,0:T(8,128)S(1)}, s32[]{:T(128)}, f32[16,16,8192]{2,1,0:T(8,128)}, f32[16,16,8192]{2,1,0:T(8,128)}, /*index=5*/s32[]{:T(128)}, s32[]{:T(128)}) while((s32[]{:T(128)}, f32[16,8192]{1,0:T(8,128)S(1)}, s32[]{:T(128)}, f32[16,16,8192]{2,1,0:T(8,128)}, f32[16,16,8192]{2,1,0:T(8,128)}, ...), condition=%wide.region_20.21_spmd.clone, body=%wide.region_19.20_spmd.clone.sunk | while | flops 524292 | bytes 2097253 | solution.py:30
  522.5 40.2 %all-gather.16.cloned.1.call-done = f32[256,8192]{1,0:T(8,128)} async-done(((f32[16,8192]{1,0:T(8,128)}), f32[256,8192]{1,0:T(8,128)}) %all-gather.16.cloned.1.call-update) | async-done | bytes 8388624 | tf_op jit(solution)/shard_map/all_gather | solution.py:18
  562.7 25.2 %while.91 = (s32[]{:T(128)}, f32[16,8192]{1,0:T(8,128)S(1)}, s32[]{:T(128)}, f32[16,16,8192]{2,1,0:T(8,128)}, f32[16,16,8192]{2,1,0:T(8,128)}, /*index=5*/s32[]{:T(128)}, s32[]{:T(128)}) while((s32[]{:T(128)}, f32[16,8192]{1,0:T(8,128)S(1)}, s32[]{:T(128)}, f32[16,16,8192]{2,1,0:T(8,128)}, f32[16,16,8192]{2,1,0:T(8,128)}, ...), condition=%wide.region_5.6_spmd.clone, body=%wide.region_4.5_spmd.clone.sunk | while | flops 524292 | bytes 2097253 | solution.py:30
  590.3 133.4 %while.89 = (s32[]{:T(128)}, f32[16,8192]{1,0:T(8,128)S(1)}, f32[16,16,8192]{2,1,0:T(8,128)}, f32[16,8,8192]{2,1,0:T(8,128)}, f32[16,8,8192]{2,1,0:T(8,128)}, /*...) while((s32[]{:T(128)}, f32[16,8192]{1,0:T(8,128)S(1)}, ...), condition=%wide.region_15.16_spmd, body=%wide.region_6.15_spmd.sunk | while | flops 9371657 | bytes 8526493 | solution.py:83
  729.7 512.2 %while.94 = (s32[]{:T(128)}, f32[16,8192]{1,0:T(8,128)S(1)}, f32[16,8192]{1,0:T(8,128)}, f32[16,8,8192]{2,1,0:T(8,128)}, f32[16,8,8192]{2,1,0:T(8,128)}, /*index...) while((s32[]{:T(128)}, f32[16,8192]{1,0:T(8,128)S(1)}, ...), condition=%wide.region_54.55_spmd.clone, body=%wide.region_21.54_spmd.clone.sunk | while | flops 28180232 | bytes 28686768 | solution.py:132
  790.4 3.8 fusion.90
  822.6 3.8 fusion.90
  854.5 3.8 fusion.90
  886.7 3.8 fusion.90
  918.3 3.8 fusion.90
  950.3 3.8 fusion.90
  982.5 3.8 fusion.90
  1014.2 3.8 fusion.90
  1046.1 3.8 fusion.90
  1077.6 3.8 fusion.90
  1109.5 3.8 fusion.90
  1141.7 3.8 fusion.90
  1173.5 3.8 fusion.90
  1205.3 3.8 fusion.90
  1238.1 3.8 fusion.90
  1242.0 12.3 fusion.55
  1255.6 4.6 fusion.56
  1260.5 4.5 convolution_convert_fusion
  1265.0 5.1 fusion.59
  1271.7 12.7 fusion.19
  1286.6 7.6 collective-permute-done.1
  1294.3 6.2 multiply_reduce_fusion.45
  1301.4 43.9 %reduce-scatter.8.cloned.1.call-done = f32[256,512]{1,0:T(8,128)} async-done(((f32[256,8192]{1,0:T(8,128)}), f32[256,512]{1,0:T(8,128)}) %reduce-scatter.8.cloned.1.call-update) | async-done | bytes 524304 | tf_op jit(solution)/shard_map/reduce_scatter | solution.py:218
  1345.3 90.5 %reduce-scatter.6.cloned.1.call-done = f32[512,288]{0,1:T(8,128)} async-done(((f32[8192,288]{0,1:T(8,128)}), f32[512,288]{0,1:T(8,128)}) %reduce-scatter.6.cloned.1.call-update) | async-done | bytes 589840 | tf_op jit(solution)/shard_map/reduce_scatter | solution.py:217
  1435.8 17.7 fusion
  1459.5 123.5 %all-reduce.7.cloned.1.call-done = (f32[8192]{0:T(1024)}, f32[8192]{0:T(1024)}, f32[8192]{0:T(1024)}) async-done(((f32[8192]{0:T(1024)}, f32[8192]{0:T(1024)}, f32[8192]{0:T(1024)}), (f32[8192]{0:T(1024)}, f32[8192]{0:T(1024)}, f32[8192]{0:T(1024)})) %all-reduce.7.cloned.1.call-update) | async-done | bytes 98320 | tf_op jit(solution)/shard_map/psum | solution.py:242
  1583.0 149.1 %all-reduce.9.cloned.1.call-done = (f32[4,8192]{1,0:T(4,128)}, f32[16,8192]{1,0:T(8,128)}) async-done(((f32[4,8192]{1,0:T(4,128)}, f32[16,8192]{1,0:T(8,128)}), (f32[4,8192]{1,0:T(4,128)}, f32[16,8192]{1,0:T(8,128)})) %all-reduce.9.cloned.1.call-update) | async-done | bytes 655376 | tf_op jit(solution)/shard_map/psum | solution.py:242
  1732.1 28.9 %reduce-scatter.10.cloned.1.call-done = f32[32,512]{1,0:T(8,128)} async-done(((f32[256,512]{1,0:T(8,128)}), f32[32,512]{1,0:T(8,128)}) %reduce-scatter.10.cloned.1.call-update) | async-done | bytes 65552 | tf_op jit(solution)/shard_map/reduce_scatter | solution.py:222
  (1337 shorter events, 770.2 us)
Async XLA Ops:
  7.2 77.0 %all-gather.10.cloned.1.call-start = ((), (), s32[]{:S(2)}) async-start(), calls=%async_computation.3 | async-start | bytes 5013504 | tf_op jit(solution)/shard_map/all_gather | solution.py:174
  23.0 120.3 %all-gather.12.cloned.1.call-start = ((), (), s32[]{:S(2)}) async-start(), calls=%async_computation.4 | async-start | bytes 4456448 | tf_op jit(solution)/shard_map/all_gather | solution.py:175
  37.2 379.4 %all-gather.18.cloned.1.call-start = ((), (), s32[]{:S(2)}) async-start(), calls=%async_computation.10 | async-start | bytes 8912896 | tf_op jit(solution)/shard_map/all_gather | solution.py:18
  38.2 8.8 collective-permute-start
  57.4 88.9 %copy-start.2 = (bf16[128,8192]{1,0:T(8,128)(2,1)}, bf16[128,8192]{1,0:T(8,128)(2,1)S(1)}, u32[]{:S(2)}) copy-start(bf16[128,8192]{1,0:T(8,128)(2,1)S(1)} %get-tuple-element.911) | copy-start | bytes 6291460
  57.4 85.9 %copy-start.44 = (f32[8192]{0:T(1024)S(1)}, f32[8192]{0:T(1024)}, u32[]{:S(2)}) copy-start(f32[8192]{0:T(1024)} %param.29) | copy-start | bytes 98308
  87.9 58.4 %copy-start.23 = (f32[128,288]{0,1:T(8,128)}, f32[128,288]{0,1:T(8,128)S(1)}, u32[]{:S(2)}) copy-start(f32[128,288]{0,1:T(8,128)S(1)} %fusion.76) | copy-start | bytes 442372
  152.9 146.0 %copy-start.21 = (f32[16,8192]{1,0:T(8,128)S(1)}, f32[16,8192]{1,0:T(8,128)}, u32[]{:S(2)}) copy-start(f32[16,8192]{1,0:T(8,128)} %param.30) | copy-start | bytes 1572868
  345.5 144.2 %all-gather.14.cloned.1.call-start = ((), (), s32[]{:S(2)}) async-start(), calls=%async_computation.8 | async-start | bytes 8912896 | tf_op jit(solution)/shard_map/all_gather | solution.py:18
  350.9 211.8 %all-gather.16.cloned.1.call-start = ((), (), s32[]{:S(2)}) async-start(), calls=%async_computation.9 | async-start | bytes 8912896 | tf_op jit(solution)/shard_map/all_gather | solution.py:18
  397.0 948.3 %reduce-scatter.8.cloned.1.call-start = ((), (), s32[]{:S(2)}) async-start(), calls=%async_computation.6 | async-start | bytes 8912896 | tf_op jit(solution)/shard_map/reduce_scatter | solution.py:218
  732.5 18.4 %copy-start.5 = (f32[1,1,8192]{2,1,0:T(1,128)}, f32[1,1,8192]{2,1,0:T(1,128)S(1)}, u32[]{:S(2)}) copy-start(f32[1,1,8192]{2,1,0:T(1,128)S(1)} %get-tuple-element.1514) | copy-start | bytes 98308 | tf_op jit(solution)/shard_map/while
  764.6 18.4 %copy-start.5 = (f32[1,1,8192]{2,1,0:T(1,128)}, f32[1,1,8192]{2,1,0:T(1,128)S(1)}, u32[]{:S(2)}) copy-start(f32[1,1,8192]{2,1,0:T(1,128)S(1)} %get-tuple-element.1514) | copy-start | bytes 98308 | tf_op jit(solution)/shard_map/while
  796.8 18.4 %copy-start.5 = (f32[1,1,8192]{2,1,0:T(1,128)}, f32[1,1,8192]{2,1,0:T(1,128)S(1)}, u32[]{:S(2)}) copy-start(f32[1,1,8192]{2,1,0:T(1,128)S(1)} %get-tuple-element.1514) | copy-start | bytes 98308 | tf_op jit(solution)/shard_map/while
  829.0 18.2 %copy-start.5 = (f32[1,1,8192]{2,1,0:T(1,128)}, f32[1,1,8192]{2,1,0:T(1,128)S(1)}, u32[]{:S(2)}) copy-start(f32[1,1,8192]{2,1,0:T(1,128)S(1)} %get-tuple-element.1514) | copy-start | bytes 98308 | tf_op jit(solution)/shard_map/while
  860.7 17.7 copy-start.6
  860.7 18.6 %copy-start.5 = (f32[1,1,8192]{2,1,0:T(1,128)}, f32[1,1,8192]{2,1,0:T(1,128)S(1)}, u32[]{:S(2)}) copy-start(f32[1,1,8192]{2,1,0:T(1,128)S(1)} %get-tuple-element.1514) | copy-start | bytes 98308 | tf_op jit(solution)/shard_map/while
  892.8 18.1 %copy-start.5 = (f32[1,1,8192]{2,1,0:T(1,128)}, f32[1,1,8192]{2,1,0:T(1,128)S(1)}, u32[]{:S(2)}) copy-start(f32[1,1,8192]{2,1,0:T(1,128)S(1)} %get-tuple-element.1514) | copy-start | bytes 98308 | tf_op jit(solution)/shard_map/while
  924.4 17.5 copy-start.6
  924.4 18.5 %copy-start.5 = (f32[1,1,8192]{2,1,0:T(1,128)}, f32[1,1,8192]{2,1,0:T(1,128)S(1)}, u32[]{:S(2)}) copy-start(f32[1,1,8192]{2,1,0:T(1,128)S(1)} %get-tuple-element.1514) | copy-start | bytes 98308 | tf_op jit(solution)/shard_map/while
  956.6 17.5 copy-start.6
  956.6 18.5 %copy-start.5 = (f32[1,1,8192]{2,1,0:T(1,128)}, f32[1,1,8192]{2,1,0:T(1,128)S(1)}, u32[]{:S(2)}) copy-start(f32[1,1,8192]{2,1,0:T(1,128)S(1)} %get-tuple-element.1514) | copy-start | bytes 98308 | tf_op jit(solution)/shard_map/while
  988.7 18.2 %copy-start.5 = (f32[1,1,8192]{2,1,0:T(1,128)}, f32[1,1,8192]{2,1,0:T(1,128)S(1)}, u32[]{:S(2)}) copy-start(f32[1,1,8192]{2,1,0:T(1,128)S(1)} %get-tuple-element.1514) | copy-start | bytes 98308 | tf_op jit(solution)/shard_map/while
  1020.3 17.5 copy-start.6
  1020.3 18.5 %copy-start.5 = (f32[1,1,8192]{2,1,0:T(1,128)}, f32[1,1,8192]{2,1,0:T(1,128)S(1)}, u32[]{:S(2)}) copy-start(f32[1,1,8192]{2,1,0:T(1,128)S(1)} %get-tuple-element.1514) | copy-start | bytes 98308 | tf_op jit(solution)/shard_map/while
  1052.2 18.0 %copy-start.5 = (f32[1,1,8192]{2,1,0:T(1,128)}, f32[1,1,8192]{2,1,0:T(1,128)S(1)}, u32[]{:S(2)}) copy-start(f32[1,1,8192]{2,1,0:T(1,128)S(1)} %get-tuple-element.1514) | copy-start | bytes 98308 | tf_op jit(solution)/shard_map/while
  1083.7 17.5 copy-start.6
  1083.7 18.5 %copy-start.5 = (f32[1,1,8192]{2,1,0:T(1,128)}, f32[1,1,8192]{2,1,0:T(1,128)S(1)}, u32[]{:S(2)}) copy-start(f32[1,1,8192]{2,1,0:T(1,128)S(1)} %get-tuple-element.1514) | copy-start | bytes 98308 | tf_op jit(solution)/shard_map/while
  1115.7 17.7 copy-start.6
  1115.7 18.7 %copy-start.5 = (f32[1,1,8192]{2,1,0:T(1,128)}, f32[1,1,8192]{2,1,0:T(1,128)S(1)}, u32[]{:S(2)}) copy-start(f32[1,1,8192]{2,1,0:T(1,128)S(1)} %get-tuple-element.1514) | copy-start | bytes 98308 | tf_op jit(solution)/shard_map/while
  1147.6 17.5 copy-start.6
  1147.7 18.5 %copy-start.5 = (f32[1,1,8192]{2,1,0:T(1,128)}, f32[1,1,8192]{2,1,0:T(1,128)S(1)}, u32[]{:S(2)}) copy-start(f32[1,1,8192]{2,1,0:T(1,128)S(1)} %get-tuple-element.1514) | copy-start | bytes 98308 | tf_op jit(solution)/shard_map/while
  1179.6 18.4 %copy-start.5 = (f32[1,1,8192]{2,1,0:T(1,128)}, f32[1,1,8192]{2,1,0:T(1,128)S(1)}, u32[]{:S(2)}) copy-start(f32[1,1,8192]{2,1,0:T(1,128)S(1)} %get-tuple-element.1514) | copy-start | bytes 98308 | tf_op jit(solution)/shard_map/while
  1211.5 18.3 %copy-start.6 = (f32[1,1,8192]{2,1,0:T(1,128)}, f32[1,1,8192]{2,1,0:T(1,128)S(1)}, u32[]{:S(2)}) copy-start(f32[1,1,8192]{2,1,0:T(1,128)S(1)} %get-tuple-element.1503) | copy-start | bytes 98308 | tf_op jit(solution)/shard_map/while
  1211.5 19.3 %copy-start.5 = (f32[1,1,8192]{2,1,0:T(1,128)}, f32[1,1,8192]{2,1,0:T(1,128)S(1)}, u32[]{:S(2)}) copy-start(f32[1,1,8192]{2,1,0:T(1,128)S(1)} %get-tuple-element.1514) | copy-start | bytes 98308 | tf_op jit(solution)/shard_map/while
  1260.2 175.6 %reduce-scatter.6.cloned.1.call-start = ((), (), s32[]{:S(2)}) async-start(), calls=%async_computation.5 | async-start | bytes 10027008 | tf_op jit(solution)/shard_map/reduce_scatter | solution.py:217
  1270.1 312.9 %all-reduce.7.cloned.1.call-start = ((), (), s32[]{:S(2)}) async-start(), calls=%async_computation.11 | async-start | bytes 196608 | tf_op jit(solution)/shard_map/psum | solution.py:242
  1270.1 24.1 %slice-start = ((s8[4456448]{0:T(1024)(128)(4,1)}), s8[4194304]{0:T(1024)(128)(4,1)S(1)}, s32[]{:S(2)}) async-start(s8[4456448]{0:T(1024)(128)(4,1)} %bitcast.541), calls=%async_computation.13 | async-start | bytes 8388608
  1271.6 22.6 %slice-start.1 = ((s8[4456448]{0:T(1024)(128)(4,1)}), s8[262144]{0:T(1024)(128)(4,1)S(1)}, s32[]{:S(2)}) async-start(s8[4456448]{0:T(1024)(128)(4,1)} %bitcast.541), calls=%async_computation.14 | async-start | bytes 524288
  1271.7 22.6 %copy-start.26 = (f32[1,8192]{1,0:T(1,128)S(1)}, f32[1,8192]{1,0:T(1,128)}, u32[]{:S(2)}) copy-start(f32[1,8192]{1,0:T(1,128)} %copy-done.25) | copy-start | bytes 98308
  1271.7 22.6 %copy-start.28 = (f32[1,8192]{1,0:T(1,128)S(1)}, f32[1,8192]{1,0:T(1,128)}, u32[]{:S(2)}) copy-start(f32[1,8192]{1,0:T(1,128)} %copy-done.27) | copy-start | bytes 98308
  1271.7 22.6 %copy-start.30 = (f32[1,8192]{1,0:T(1,128)S(1)}, f32[1,8192]{1,0:T(1,128)}, u32[]{:S(2)}) copy-start(f32[1,8192]{1,0:T(1,128)} %copy-done.29) | copy-start | bytes 98308
  1271.7 22.6 %copy-start.32 = (f32[1,8192]{1,0:T(1,128)S(1)}, f32[1,8192]{1,0:T(1,128)}, u32[]{:S(2)}) copy-start(f32[1,8192]{1,0:T(1,128)} %copy-done.31) | copy-start | bytes 98308
  1284.4 9.8 collective-permute-start.1
  1286.6 169.9 %copy-start.46 = (u32[128]{0:T(128)S(1)}, u32[128]{0:T(128)}, u32[]{:S(2)}) copy-start(u32[128]{0:T(128)} %constant.164) | copy-start | bytes 1540
  1300.5 431.6 %all-reduce.9.cloned.1.call-start = ((), (), s32[]{:S(2)}) async-start(), calls=%async_computation.12 | async-start | bytes 1310720 | tf_op jit(solution)/shard_map/psum | solution.py:242
  1301.4 459.7 %reduce-scatter.10.cloned.1.call-start = ((), (), s32[]{:S(2)}) async-start(), calls=%async_computation.7 | async-start | bytes 589824 | tf_op jit(solution)/shard_map/reduce_scatter | solution.py:222
  1453.6 5.1 collective-permute-start.2
  (284 other events, 2563.3 us)
Sparse Core Ops, SparseCore 0:
  23.1 60.9 all-gather.9
  86.3 56.9 all-gather.11
  345.6 70.9 all-gather.17
  419.2 70.4 all-gather.13
  492.2 70.4 all-gather.15
  1260.3 84.9 reduce-scatter.7
  1348.8 86.9 reduce-scatter.5
  1443.1 139.8 all-reduce.6
  1589.0 143.0 all-reduce.8
  1734.9 26.0 reduce-scatter.9
where the time goes:
time: 1800 us; the launch traced here: 1780 us
  waiting for transfers between devices  652 us (36%)
  other arithmetic  583 us (32%)
  local copies, waits for them, and re-layouts  431 us (24%)
  blocking collectives  46.8 us (3%)
  matrix products  33.4 us (2%)
    psum x2, waiting for transfers between devices, local(): lax.psum((grad_conv_w, grad_conv_b, grad_bias, grad_alog, grad_skip), ('d...  273 us
    another operation x1, other arithmetic, local(): cumul = jnp.cumsum(step_size, axis=0)  144 us
    reduce_sum x48, other arithmetic, retreat(): c_grads.append(jnp.sum(updated * g_blk[offset][None, :], axis=1))  128 us
    all_gather x3, waiting for transfers between devices, carried_in(): pieces = jax.tree.map(lambda part: lax.all_gather(part, axis), value)  125 us
    reduce_scatter x1, waiting for transfers between devices, local(): lax.psum_scatter(g_wx_full, 'seq', scatter_dimension=0, tiled=True)  90.5 us
    reduce_sum x64, other arithmetic, retreat(): b_grads.append(jnp.sum(adjoint * drive_blk[offset][None, :], axis=1))  84.4 us
    another operation x64, local copies, waits for them, and re-layouts, retreat(): jnp.stack(collected[::-1])  62.7 us
    add x16, other arithmetic, retreat(): rate_grad = rate_grad + moment * step_blk[offset][None, :]  60.9 us
  transfers between devices with their start and end apart: 13, of which 12 were waited for; matrix products, arithmetic and copies ran while one was open for 9% of the time, Pallas kernels for 0%

commit v1 on v0

v1 whole, which is shorter than its diff:
```python
import functools

import jax
import jax.numpy as jnp
from jax import lax
from jax.experimental import pallas as pl
from jax.experimental.pallas import tpu as pltpu
from jax.sharding import PartitionSpec as P

T = 128
N = 16
LN2 = 0.6931471805599453
LOG2E = 1.4426950408889634


def local_scan_kernel(low_ref, w_ref, x_ref, z_ref, g_ref, bias_ref, a2_ref, bc_ref,
              step_ref, drive_ref, gs_ref, sig_ref, ends_ref, tot_ref, scr):
    low = low_ref[...]
    for half in range(2):
        dt = w_ref[half, :, 48:, :].reshape(256, 512)
        cols = pl.ds(512 * half, 512)
        rate = jnp.dot(low, dt, preferred_element_type=jnp.float32) + bias_ref[:, cols]
        e = jnp.exp(-jnp.abs(rate))
        step = jnp.maximum(rate, 0.0) + jnp.log1p(e)
        sig_ref[:, cols] = jnp.where(rate >= 0, 1.0, e) / (1.0 + e)
        xw = x_ref[:, cols].astype(jnp.float32)
        z = z_ref[:, cols].astype(jnp.float32)
        gs = g_ref[:, cols].astype(jnp.float32) * (z * jax.nn.sigmoid(z))
        drive = step * xw
        for s in range(4):
            part = slice(128 * s, 128 * s + 128)
            step_ref[:, 4 * half + s, :] = step[:, part]
            drive_ref[:, 4 * half + s, :] = drive[:, part]
            gs_ref[:, 4 * half + s, :] = gs[:, part]

    def body(t, carry):
        tot, ends, prods, lams = carry
        st = step_ref[t]
        dr = drive_ref[t]
        gv = gs_ref[t]
        ne, np_, nl = [], [], []
        for n in range(N):
            f = jnp.exp2(st * a2_ref[n])
            b = bc_ref[n, pl.ds(t, 1), :]
            c = bc_ref[N + n, pl.ds(t, 1), :]
            ne.append(f * ends[n] + b * dr)
            p = prods[n] * f
            np_.append(p)
            nl.append(lams[n] + p * (c * gv))
        return tot + st, tuple(ne), tuple(np_), tuple(nl)

    zero = jnp.zeros((8, 128), jnp.float32)
    one = jnp.ones((8, 128), jnp.float32)
    tot, ends, prods, lams = lax.fori_loop(0, T, body, (zero, (zero,) * N, (one,) * N, (zero,) * N))
    for n in range(N):
        for half in range(2):
            scr[half, 4 * n:4 * n + 4, :] = ends[n][4 * half:4 * half + 4]
            scr[half, 64 + 4 * n:64 + 4 * n + 4, :] = lams[n][4 * half:4 * half + 4]
    ends_ref[...] = scr[...].astype(jnp.bfloat16)
    for half in range(2):
        tot_ref[half, 0:4, :] = tot[4 * half:4 * half + 4]
        tot_ref[half, 4:8, :] = jnp.zeros((4, 128), jnp.float32)

def local_scan(low, wg, x_conv, z, g, bias, a2, bc):
    E = x_conv.shape[1]; C = E // 1024
    nat = pl.BlockSpec((T, 1024), lambda i: (0, i))
    tri = pl.BlockSpec((T, 8, 128), lambda i: (0, i, 0))
    full = lambda shape: pl.BlockSpec(shape, lambda i: (0,) * len(shape))
    f32 = jnp.float32
    return pl.pallas_call(
        local_scan_kernel, grid=(C,), name="local_scan",
        in_specs=[full((T, 256)), pl.BlockSpec((2, 8, 80, 512), lambda i: (i, 0, 0, 0)), nat, nat, nat,
                  pl.BlockSpec((1, 1024), lambda i: (0, i)), pl.BlockSpec((N, 8, 128), lambda i: (0, i, 0)),
                  full((32, T, 128))],
        out_specs=[tri, tri, tri, nat, pl.BlockSpec((2, 128, 128), lambda i: (i, 0, 0)), pl.BlockSpec((2, 8, 128), lambda i: (i, 0, 0))],
        out_shape=[jax.ShapeDtypeStruct((T, E // 128, 128), f32)] * 3 + [jax.ShapeDtypeStruct((T, E), f32),
                   jax.ShapeDtypeStruct((2 * C, 128, 128), jnp.bfloat16), jax.ShapeDtypeStruct((2 * C, 8, 128), f32)],
        scratch_shapes=[pltpu.VMEM((2, 128, 128), f32)],
        compiler_params=pltpu.CompilerParams(vmem_limit_bytes=60 * 2**20),
    )(low, wg, x_conv, z, g, bias, a2, bc)

def main_scan_kernel(step_ref, drive_ref, gs_ref, sig_ref, x_ref, z_ref, g_ref, dskip_ref, a2_ref, bc_ref, ent_ref, w_ref, low_ref,
              mix_ref, gz_ref, gcx_ref, gdt_ref, par_ref, ga_ref, glow_ref, gbc_ref,
              es, us, fs, y3, gd3, gr3, accb, accc, alow):
    i = pl.program_id(0)
    f32 = jnp.float32

    @pl.when(i == 0)
    def _():
        accb[...] = jnp.zeros(accb.shape, f32)
        accc[...] = jnp.zeros(accc.shape, f32)
        alow[...] = jnp.zeros(alow.shape, f32)

    es[...] = ent_ref[...].astype(f32)

    def state(base, n):
        return jnp.concatenate([es[0, base + 4 * n:base + 4 * n + 4, :], es[1, base + 4 * n:base + 4 * n + 4, :]], axis=0)

    def forward(t, hs):
        st, dr, gv = step_ref[t], drive_ref[t], gs_ref[t]
        new = []
        y = None
        for n in range(N):
            f = jnp.exp2(st * a2_ref[n])
            u = f * hs[n]
            fs[t, n] = f
            us[t, n] = u
            h = u + bc_ref[n, pl.ds(t, 1), :] * dr
            new.append(h)
            ch = bc_ref[N + n, pl.ds(t, 1), :] * h
            y = ch if y is None else y + ch
            accc[t, n] += h * gv
        y3[t] = y
        return tuple(new)

    lax.fori_loop(0, T, forward, tuple(state(0, n) for n in range(N)))

    def backward(k, carry):
        adj, ra = carry
        t = T - 1 - k
        st, dr, gv = step_ref[t], drive_ref[t], gs_ref[t]
        na, nr = [], []
        gd = gr = None
        for n in range(N):
            lam = bc_ref[N + n, pl.ds(t, 1), :] * gv + adj[n]
            lb = lam * bc_ref[n, pl.ds(t, 1), :]
            accb[t, n] += lam * dr
            na.append(fs[t, n] * lam)
            m = lam * us[t, n]
            ma = m * a2_ref[n]
            nr.append(ra[n] + m * st)
            gd = lb if gd is None else gd + lb
            gr = ma if gr is None else gr + ma
        gd3[t] = gd
        gr3[t] = gr
        return tuple(na), tuple(nr)

    zero = jnp.zeros((8, 128), f32)
    adj, ra = lax.fori_loop(0, T, backward, (tuple(state(64, n) for n in range(N)), (zero,) * N))
    for n in range(N):
        ga_ref[n] = ra[n] * a2_ref[n] * LN2

    for half in range(2):
        dt = w_ref[half, :, 48:, :].reshape(256, 512)
        gpb = []
        for s4 in range(4):
            s = 4 * half + s4
            cols = slice(128 * s, 128 * s + 128)
            xw = x_ref[:, cols].astype(f32)
            z = z_ref[:, cols].astype(f32)
            gw = g_ref[:, cols].astype(f32)
            dsk = dskip_ref[:, cols]
            sz = jax.nn.sigmoid(z)
            inner = y3[:, s, :] + dsk * xw
            mix_ref[:, cols] = (z * sz * inner).astype(jnp.bfloat16)
            gz_ref[:, cols] = (gw * inner * (sz * (1.0 + z * (1.0 - sz)))).astype(jnp.bfloat16)
            gsn = gw * (z * sz)
            gd = gd3[:, s, :]
            gpre = (gd * xw + gr3[:, s, :] * LN2) * sig_ref[:, cols]
            gcx_ref[:, cols] = gd * step_ref[:, s, :] + gsn * dsk
            par_ref[0:1, cols] = jnp.sum(gpre, axis=0, keepdims=True)
            par_ref[1:2, cols] = jnp.sum(gsn * xw, axis=0, keepdims=True)
            gpb.append(gpre.astype(jnp.bfloat16))
        gp = jnp.concatenate(gpb, axis=1)
        alow[...] += lax.dot_general(gp, dt, (((1,), (1,)), ((), ())), preferred_element_type=f32)
        gdt_ref[half] = lax.dot_general(low_ref[...], gp, (((0,), (0,)), ((), ())),
                                        preferred_element_type=f32).reshape(8, 32, 512).astype(jnp.bfloat16)

    @pl.when(i == pl.num_programs(0) - 1)
    def _():
        glow_ref[...] = alow[...]

        def fold(t, _):
            gbc_ref[t, 0:16, :] = jnp.sum(accb[t], axis=1)
            gbc_ref[t, 16:32, :] = jnp.sum(accc[t], axis=1)
            return 0
        lax.fori_loop(0, T, fold, 0)

def main_scan(step3, drive3, gs3, sig, x_conv, z, g, dskip, a2, bc, ent, wg, low):
    E = x_conv.shape[1]; C = E // 1024
    f32 = jnp.float32
    nat = pl.BlockSpec((T, 1024), lambda i: (0, i))
    tri = pl.BlockSpec((T, 8, 128), lambda i: (0, i, 0))
    full = lambda shape: pl.BlockSpec(shape, lambda i: (0,) * len(shape))
    S = jax.ShapeDtypeStruct
    return pl.pallas_call(
        main_scan_kernel, grid=(C,), name="main_scan",
        in_specs=[tri, tri, tri, nat, nat, nat, nat, pl.BlockSpec((1, 1024), lambda i: (0, i)),
                  pl.BlockSpec((N, 8, 128), lambda i: (0, i, 0)), full((32, T, 128)),
                  pl.BlockSpec((2, 128, 128), lambda i: (i, 0, 0)),
                  pl.BlockSpec((2, 8, 80, 512), lambda i: (i, 0, 0, 0)), full((T, 256))],
        out_specs=[nat, nat, nat, pl.BlockSpec((2, 8, 32, 512), lambda i: (i, 0, 0, 0)),
                   pl.BlockSpec((8, 1024), lambda i: (0, i)), pl.BlockSpec((N, 8, 128), lambda i: (0, i, 0)),
                   full((T, 256)), full((T, 32, 128))],
        out_shape=[S((T, E), jnp.bfloat16), S((T, E), jnp.bfloat16), S((T, E), f32), S((2 * C, 8, 32, 512), jnp.bfloat16),
                   S((8, E), f32), S((N, E // 128, 128), f32), S((T, 256), f32), S((T, 32, 128), f32)],
        scratch_shapes=[pltpu.VMEM((2, 128, 128), f32), pltpu.VMEM((T, N, 8, 128), f32), pltpu.VMEM((T, N, 8, 128), f32),
                        pltpu.VMEM((T, 8, 128), f32), pltpu.VMEM((T, 8, 128), f32), pltpu.VMEM((T, 8, 128), f32),
                        pltpu.VMEM((T, N, 8, 128), f32), pltpu.VMEM((T, N, 8, 128), f32), pltpu.VMEM((T, 256), f32)],
        compiler_params=pltpu.CompilerParams(vmem_limit_bytes=62 * 2**20),
    )(step3, drive3, gs3, sig, x_conv, z, g, dskip, a2, bc, ent, wg, low)


MESH = pl.DeviceIdType.MESH
ORDERS = (("x", "y", "z"), ("y", "z", "x"), ("z", "x", "y"))
ROWS = ((0, 32), (32, 32), (64, 16))
DIMS = {"z": 0, "x": 1, "y": 2}


def place():
    d, j = lax.axis_index("dp"), lax.axis_index("seq")
    return d, j, {"z": lax.div(j, 4), "x": lax.rem(j, 4), "y": lax.div(d, 2)}, lax.rem(d, 2)


def peer(pos, core, axis, hop):
    at = dict(pos)
    at[axis] = lax.rem(at[axis] + hop + 4, 4)
    return (at["y"] * 2 + core, at["z"] * 4 + at["x"])


def greet(devices):
    barrier = pltpu.get_barrier_semaphore()
    for device in devices:
        pl.semaphore_signal(barrier, inc=1, device_id=device, device_id_type=MESH)
    pl.semaphore_wait(barrier, len(devices))


def remote(src, dst, send_sem, recv_sem, device):
    return pltpu.make_async_remote_copy(
        src_ref=src, dst_ref=dst, send_sem=send_sem, recv_sem=recv_sem, device_id=device, device_id_type=MESH
    )


def slab(ref, fixed, tail):
    index = [slice(None)] * 3
    for axis, value in fixed.items():
        index[DIMS[axis]] = value
    return ref.at[tuple(index) + tail]


def gather_kernel(parts, with_tail, *refs):
    if with_tail:
        shard, tail_ref, out, halo, local_sem, ssem, rsem, csend, crecv, hsend, hrecv = refs
    else:
        shard, out, local_sem, ssem, rsem, csend, crecv = refs
    d, j, pos, core = place()
    sibling = (pos["y"] * 2 + 1 - core, j)
    following, previous = (d, lax.rem(j + 1, 16)), (d, lax.rem(j + 15, 16))
    near = [peer(pos, core, axis, hop) for axis in "xyz" for hop in (1, -1)]
    greet(near + [sibling] + ([previous] if with_tail else []))
    sent = []

    def go(copy):
        copy.start()
        sent.append(copy)

    if with_tail:
        tail_copy = remote(tail_ref, halo, hsend, hrecv, following)
        go(tail_copy)
    own = out.at[pos["z"], pos["x"], pos["y"], core]
    local = pltpu.make_async_copy(shard, own, local_sem)
    local.start()
    local.wait()

    def step(p, stage):
        order, (row, count) = parts[p]
        axis = order[stage]
        done = order[:stage]
        fixed = {a: pos[a] for a in "xyz" if a not in done}
        rows = pl.ds(row, count)
        half = out.shape[-1] // 2
        columns = (pl.ds(0, half), pl.ds(half, half))
        right, left = peer(pos, core, axis, 1), peer(pos, core, axis, -1)

        def at(hop, cols=slice(None)):
            return slab(out, {**fixed, axis: lax.rem(pos[axis] + hop + 4, 4)}, (core, rows, cols))

        def copy(which):
            hop, cols, device = ((0, slice(None), right), (0, slice(None), left),
                                 (-1, columns[0], right), (1, columns[1], left))[which]
            return remote(at(hop, cols), at(hop, cols), ssem.at[p, stage, which], rsem.at[p, stage, which], device)

        def landed(which):
            hop, cols, device = ((-1, slice(None), right), (1, slice(None), left),
                                 (2, columns[0], right), (2, columns[1], left))[which]
            remote(at(hop, cols), at(hop, cols), ssem.at[p, stage, which], rsem.at[p, stage, which], device).wait_recv()

        def across(which):
            hop = (0, -1, 1, 2)[which]
            return remote(at(hop), at(hop), csend.at[p, which], crecv.at[p, which], sibling)

        def crossed(which):
            hop = (0, -1, 1, 2)[which]
            there = slab(out, {**fixed, axis: lax.rem(pos[axis] + hop + 4, 4)}, (1 - core, rows, slice(None)))
            remote(there, there, csend.at[p, which], crecv.at[p, which], sibling).wait_recv()

        return copy, landed, across, crossed

    count = len(parts)
    for stage in range(3):
        steps = [step(p, stage) for p in range(count)]
        for copy, landed, across, crossed in steps:
            go(copy(0))
            go(copy(1))
            if stage == 2:
                go(across(0))
        for which in (0, 1):
            for copy, landed, across, crossed in steps:
                landed(which)
                go(copy(2 + which))
                if stage == 2:
                    go(across(1 + which))
        for copy, landed, across, crossed in steps:
            landed(2)
            landed(3)
            if stage == 2:
                go(across(3))
    for copy, landed, across, crossed in steps:
        for which in range(4):
            crossed(which)
    if with_tail:
        tail_copy.wait_recv()
    for copy in sent:
        copy.wait_send()


def gather(shard, tail, parts, collective_id):
    rows, columns = shard.shape
    count = len(parts)
    anyspace = pl.BlockSpec(memory_space=pl.ANY)
    dma = pltpu.SemaphoreType.DMA
    out_shape = [jax.ShapeDtypeStruct((4, 4, 4, 2, rows, columns), shard.dtype)]
    sems = [dma, dma((count, 3, 4)), dma((count, 3, 4)), dma((count, 4)), dma((count, 4))]
    operands = [shard]
    if tail is not None:
        out_shape.append(jax.ShapeDtypeStruct(tail.shape, tail.dtype))
        sems += [dma, dma]
        operands.append(tail)
    return pl.pallas_call(
        functools.partial(gather_kernel, parts, tail is not None),
        name="gather_shards",
        out_shape=out_shape,
        in_specs=[anyspace] * len(operands),
        out_specs=[anyspace] * len(out_shape),
        scratch_shapes=sems,
        compiler_params=pltpu.CompilerParams(collective_id=collective_id, has_side_effects=True),
    )(*operands)


def carry_kernel(ends, tot, a2, out, got, got_tot, back, ssem, rsem, tsend, trecv, bsend, brecv):
    d, j, pos, core = place()
    peers = [(d, lax.rem(j + k, 16)) for k in range(1, 16)]
    greet(peers)
    sent = []
    for k in range(1, 16):
        to = lax.rem(j + k, 16)
        one = remote(ends.at[to], got.at[j], ssem.at[k], rsem.at[k], peers[k - 1])
        two = remote(tot.at[to], got_tot.at[j], tsend.at[k], trecv.at[k], peers[k - 1])
        one.start()
        two.start()
        sent += [one, two]
    got[j] = ends[j]
    got_tot[j] = tot[j]
    for k in range(1, 16):
        source = lax.rem(j + 16 - k, 16)
        remote(got.at[source], got.at[source], ssem.at[k], rsem.at[k], peers[k - 1]).wait_recv()
        remote(got_tot.at[source], got_tot.at[source], tsend.at[k], trecv.at[k], peers[k - 1]).wait_recv()
    rates = a2[j]

    def decay(i):
        return jnp.exp2(rates * jnp.concatenate([got_tot[i, 0:4, :]] * 16, axis=0))

    enter = jnp.zeros((64, 128), jnp.float32)
    leave = jnp.zeros((64, 128), jnp.float32)
    for i in range(16):
        back[i, 0:64, :] = enter.astype(jnp.bfloat16)
        enter = decay(i) * enter + got[i, 0:64, :].astype(jnp.float32)
        r = 15 - i
        back[r, 64:128, :] = leave.astype(jnp.bfloat16)
        leave = decay(r) * leave + got[r, 64:128, :].astype(jnp.float32)
    for k in range(1, 16):
        to = lax.rem(j + k, 16)
        one = remote(back.at[to], out.at[j], bsend.at[k], brecv.at[k], peers[k - 1])
        one.start()
        sent.append(one)
    out[j] = back[j]
    for k in range(1, 16):
        source = lax.rem(j + 16 - k, 16)
        remote(out.at[source], out.at[source], bsend.at[k], brecv.at[k], peers[k - 1]).wait_recv()
    for copy in sent:
        copy.wait_send()


def carry(ends, tot, a2):
    vmem = pl.BlockSpec(memory_space=pltpu.VMEM)
    dma = pltpu.SemaphoreType.DMA((16,))
    return pl.pallas_call(
        carry_kernel,
        name="carry_exchange",
        out_shape=jax.ShapeDtypeStruct((16, 128, 128), jnp.bfloat16),
        in_specs=[vmem] * 3,
        out_specs=vmem,
        scratch_shapes=[
            pltpu.VMEM((16, 128, 128), jnp.bfloat16),
            pltpu.VMEM((16, 8, 128), jnp.float32),
            pltpu.VMEM((16, 128, 128), jnp.bfloat16),
            dma, dma, dma, dma, dma, dma,
        ],
        compiler_params=pltpu.CompilerParams(
            collective_id=1, has_side_effects=True, vmem_limit_bytes=32 * 2**20
        ),
    )(ends, tot, a2)


def reduce_kernel(part_ref, edge, out, all_params, halo, sums, cross, *scratch):
    buffers, scratch = scratch[:36], scratch[36:]
    packed, csend, crecv, ssem, rsem, psend, precv, pcs, pcr, hsend, hrecv = scratch
    d, j, pos, core = place()
    sibling = (pos["y"] * 2 + 1 - core, j)
    following, previous = (d, lax.rem(j + 1, 16)), (d, lax.rem(j + 15, 16))
    near = [peer(pos, core, axis, hop) for axis in "xyz" for hop in (1, -1)]
    greet(near + [sibling, following])
    sent = []

    def go(copy):
        copy.start()
        sent.append(copy)

    def across(p):
        row, count = ROWS[p]
        there = cross.at[:, :, :, pl.ds(row, count), :]
        return remote(part_ref.at[:, :, :, 1 - core, pl.ds(row, count), :], there, csend.at[p], crecv.at[p], sibling)

    for p in range(3):
        go(across(p))
    edge_copy = remote(edge, halo, hsend, hrecv, previous)
    go(edge_copy)
    for p in range(3):
        row, count = ROWS[p]
        rows = pl.ds(row, count)
        across(p).wait_recv()

        def add_core(i, _):
            a, b, c = lax.div(i, 16), lax.rem(lax.div(i, 4), 4), lax.rem(i, 4)
            sums[a, b, c, rows, :] = (
                part_ref[a, b, c, core, rows, :].astype(jnp.float32) + cross[a, b, c, rows, :].astype(jnp.float32)
            ).astype(jnp.bfloat16)
            return 0

        lax.fori_loop(0, 64, add_core, 0)

    def step(p, stage):
        order, (row, count) = ORDERS[p], ROWS[p]
        axis = order[2 - stage]
        fixed = {a: pos[a] for a in order[3 - stage:]}
        rows = pl.ds(row, count)
        half = 256
        columns = (slice(0, half), slice(half, 2 * half))
        right, left = peer(pos, core, axis, 1), peer(pos, core, axis, -1)
        bufs = buffers[(p * 3 + stage) * 4:(p * 3 + stage) * 4 + 4]
        free = [a for a in ("z", "x", "y") if a not in fixed and a != axis]

        def spot(hop):
            return lax.rem(pos[axis] + hop + 4, 4)

        def copy(which):
            hop, cols, device = ((2, columns[0], right), (2, columns[1], left),
                                 (1, slice(None), right), (-1, slice(None), left))[which]
            source = slab(sums, {**fixed, axis: spot(hop)}, (rows, cols))
            return remote(source, bufs[which], ssem.at[p, stage, which], rsem.at[p, stage, which], device)

        def add(hop, cols, terms):
            def at(values):
                index = [None] * 3
                for a, v in {**fixed, axis: spot(hop), **dict(zip(free, values))}.items():
                    index[DIMS[a]] = v
                return tuple(index) + (rows, cols)

            def one(i, _):
                values = (lax.div(i, 4), lax.rem(i, 4))[2 - len(free):] if free else ()
                total = sums[at(values)].astype(jnp.float32)
                for term in terms:
                    total = total + term[tuple(values)].astype(jnp.float32)
                sums[at(values)] = total.astype(jnp.bfloat16)
                return 0

            if free:
                lax.fori_loop(0, 4 ** len(free), one, 0)
            else:
                total = sums[at(())].astype(jnp.float32)
                for term in terms:
                    total = total + term[...].astype(jnp.float32)
                out[rows, :] = total

        def add_half(which):
            cols, hop = columns[which], (1, -1)[which]

            def at(values):
                index = [None] * 3
                for a, v in {**fixed, axis: spot(hop), **dict(zip(free, values))}.items():
                    index[DIMS[a]] = v
                return tuple(index) + (rows, cols)

            def one(i, _):
                values = (lax.div(i, 4), lax.rem(i, 4))[2 - len(free):] if free else ()
                mine = sums[at(values)].astype(jnp.float32)
                sums[at(values)] = (mine + bufs[which][tuple(values) if free else ...].astype(jnp.float32)).astype(jnp.bfloat16)
                return 0

            if free:
                lax.fori_loop(0, 4 ** len(free), one, 0)
            else:
                one(0, 0)

        return copy, (lambda which: copy(which).wait_recv()), add_half, (lambda: add(0, slice(None), bufs[2:]))

    for stage in range(3):
        steps = [step(p, stage) for p in range(3)]
        for copy, landed, add_half, finish in steps:
            go(copy(0))
            go(copy(1))
        for which in (0, 1):
            for copy, landed, add_half, finish in steps:
                landed(which)
                add_half(which)
                go(copy(2 + which))
        for copy, landed, add_half, finish in steps:
            landed(2)
            landed(3)
            finish()

    packed[...] = jnp.zeros((16, 128), jnp.bfloat16)
    rowsum = jnp.concatenate(
        [out[36 + q:37 + q, 128 * s:128 * s + 128] for q in range(3) for s in range(4)] + [jnp.zeros((4, 128), jnp.float32)], axis=0
    )
    packed[...] = rowsum.astype(jnp.bfloat16)
    all_params[pos["z"], pos["x"], pos["y"], core] = packed[...]
    order = ("y", "z", "x")
    for stage in range(3):
        axis = order[stage]
        fixed = {a: pos[a] for a in order[stage:]}

        def block(hop):
            return slab(all_params, {**fixed, axis: lax.rem(pos[axis] + hop + 4, 4)}, (core,))

        def send(which):
            hop, device = ((0, peer(pos, core, axis, 1)), (0, peer(pos, core, axis, -1)), (-1, peer(pos, core, axis, 1)))[which]
            return remote(block(hop), block(hop), psend.at[stage, which], precv.at[stage, which], device)

        def arrive(which):
            hop, device = ((-1, peer(pos, core, axis, 1)), (1, peer(pos, core, axis, -1)), (2, peer(pos, core, axis, 1)))[which]
            remote(block(hop), block(hop), psend.at[stage, which], precv.at[stage, which], device).wait_recv()

        go(send(0))
        go(send(1))
        arrive(0)
        go(send(2))
        arrive(1)
        arrive(2)
    mine, theirs = all_params.at[:, :, :, core], all_params.at[:, :, :, 1 - core]
    go(remote(mine, mine, pcs, pcr, sibling))
    remote(theirs, theirs, pcs, pcr, sibling).wait_recv()
    edge_copy.wait_recv()
    for copy in sent:
        copy.wait_send()


def reduce_all(part, edge):
    vmem = pl.BlockSpec(memory_space=pltpu.VMEM)
    anyspace = pl.BlockSpec(memory_space=pl.ANY)
    dma = pltpu.SemaphoreType.DMA
    bf16 = jnp.bfloat16
    buffers = []
    for row, count in ROWS:
        for stage in range(3):
            lead = (4,) * (2 - stage)
            buffers += [pltpu.VMEM(lead + (count, 256), bf16)] * 2 + [pltpu.VMEM(lead + (count, 512), bf16)] * 2
    return pl.pallas_call(
        reduce_kernel,
        name="reduce_shards",
        out_shape=[
            jax.ShapeDtypeStruct((80, 512), jnp.float32),
            jax.ShapeDtypeStruct((4, 4, 4, 2, 16, 128), bf16),
            jax.ShapeDtypeStruct(edge.shape, edge.dtype),
        ],
        in_specs=[vmem, anyspace],
        out_specs=[vmem, vmem, anyspace],
        scratch_shapes=[pltpu.VMEM((4, 4, 4, 80, 512), bf16)] * 2 + buffers + [
            pltpu.VMEM((16, 128), bf16),
            dma((3,)), dma((3,)), dma((3, 3, 4)), dma((3, 3, 4)), dma((3, 3)), dma((3, 3)), dma, dma, dma, dma,
        ],
        compiler_params=pltpu.CompilerParams(
            collective_id=2, has_side_effects=True, vmem_limit_bytes=48 * 2**20
        ),
    )(part, edge)


def tile_specs(width):
    nat = pl.BlockSpec((T, width), lambda i: (0, i))
    row = lambda count: pl.BlockSpec((count, width), lambda i: (0, i))
    full = lambda *shape: pl.BlockSpec(shape, lambda i: (0,) * len(shape))
    return nat, row, full


def spread(rows, columns, row_is_plain):
    plain = lax.broadcasted_iota(jnp.int32, (rows, columns), 0 if row_is_plain else 1)
    padded = lax.broadcasted_iota(jnp.int32, (rows, columns), 1 if row_is_plain else 0)
    device = lax.div(padded, 48)
    inside = padded - 48 * device
    return jnp.where((inside < 36) & (36 * device + inside == plain), 1.0, 0.0).astype(jnp.bfloat16)


def conv_kernel(x_ref, halo_ref, cw_ref, cb_ref, w_ref, xc_ref, slope_ref, low_ref, bc_ref, ext, acc):
    i = pl.program_id(0)

    @pl.when(i == 0)
    def _():
        acc[...] = jnp.zeros(acc.shape, jnp.float32)

    first = lax.axis_index("seq") == 0
    tail = halo_ref[...].astype(jnp.float32)
    ext[0:8, :] = jnp.where(first, 0.0, tail[8:16])
    ext[8:T + 8, :] = x_ref[...].astype(jnp.float32)
    for half in range(2):
        cols = slice(512 * half, 512 * half + 512)
        pre = cb_ref[:, cols] + cw_ref[0:1, cols] * ext[5:5 + T, cols]
        for k in range(1, 4):
            pre = pre + cw_ref[k:k + 1, cols] * ext[5 + k:5 + k + T, cols]
        logistic = jax.nn.sigmoid(pre)
        slope_ref[:, cols] = logistic * (1.0 + pre * (1.0 - logistic))
        xc = (pre * logistic).astype(jnp.bfloat16)
        xc_ref[:, cols] = xc
        acc[...] += lax.dot_general(
            xc, w_ref[half, :, 0:48, :].reshape(384, 512), (((1,), (1,)), ((), ())), preferred_element_type=jnp.float32
        )

    @pl.when(i == pl.num_programs(0) - 1)
    def _():
        low_ref[...] = jnp.dot(
            acc[...].astype(jnp.bfloat16), spread(384, 256, False), preferred_element_type=jnp.float32
        ).astype(jnp.bfloat16)
        for n in range(32):
            bc_ref[n] = jnp.broadcast_to(acc[:, 340 + n:341 + n], (T, 128))


def conv_project(x, halo, cw, cb, wg):
    E = x.shape[1]
    nat, row, full = tile_specs(1024)
    S = jax.ShapeDtypeStruct
    return pl.pallas_call(
        conv_kernel, grid=(E // 1024,), name="conv_project",
        in_specs=[nat, row(16), row(4), row(1), pl.BlockSpec((2, 8, 80, 512), lambda i: (i, 0, 0, 0))],
        out_specs=[nat, nat, full(T, 256), full(32, T, 128)],
        out_shape=[S((T, E), jnp.bfloat16), S((T, E), jnp.float32), S((T, 256), jnp.bfloat16), S((32, T, 128), jnp.float32)],
        scratch_shapes=[pltpu.VMEM((T + 8, 1024), jnp.float32), pltpu.VMEM((T, 384), jnp.float32)],
        compiler_params=pltpu.CompilerParams(vmem_limit_bytes=48 * 2**20),
    )(x, halo, cw, cb, wg)


def grads_kernel(glow_ref, gbc_ref, gcx_ref, slope_ref, xc_ref, x_ref, halo_ref, w_ref, gdt_ref, par_ref, ga_ref,
                 gconv_ref, part_ref, gproj, ext, wide):
    i = pl.program_id(0)
    f32 = jnp.float32

    @pl.when(i == 0)
    def _():
        plain = jnp.concatenate([glow_ref[...], gbc_ref[...]], axis=1).astype(jnp.bfloat16)
        gproj[...] = jnp.dot(plain, spread(288, 384, True), preferred_element_type=f32).astype(jnp.bfloat16)

    first = lax.axis_index("seq") == 0
    tail = halo_ref[...].astype(f32)
    ext[0:8, :] = jnp.where(first, 0.0, tail[8:16])
    ext[8:T + 8, :] = x_ref[...].astype(f32)
    for half in range(2):
        cols = slice(512 * half, 512 * half + 512)
        weights = w_ref[half, :, 0:48, :].reshape(384, 512)
        g_conv = (gcx_ref[:, cols] + jnp.dot(gproj[...], weights, preferred_element_type=f32)) * slope_ref[:, cols]
        gconv_ref[:, cols] = g_conv
        wide[...] = lax.dot_general(gproj[...], xc_ref[:, cols], (((0,), (0,)), ((), ())), preferred_element_type=f32)

        def put(r, value):
            wide[48 * (r // 3) + 36 + r % 3:48 * (r // 3) + 37 + r % 3, :] = value

        for k in range(4):
            put(k, jnp.sum(g_conv * ext[5 + k:5 + k + T, cols], axis=0, keepdims=True))
        put(4, jnp.sum(g_conv, axis=0, keepdims=True))
        put(5, par_ref[0:1, cols])
        put(6, par_ref[1:2, cols])
        for n in range(N):
            put(7 + n, jnp.concatenate([ga_ref[n, 4 * half + s:4 * half + s + 1, :] for s in range(4)], axis=1))
        part_ref[half, :, 0:48, :] = wide[...].reshape(8, 48, 512).astype(jnp.bfloat16)
        part_ref[half, :, 48:80, :] = gdt_ref[half]


def weight_grads(glow, gbc, gcx, slope, xc, x, halo, wg, gdt, par, ga):
    E = x.shape[1]
    nat, row, full = tile_specs(1024)
    S = jax.ShapeDtypeStruct
    block = pl.BlockSpec((2, 8, 80, 512), lambda i: (i, 0, 0, 0))
    return pl.pallas_call(
        grads_kernel, grid=(E // 1024,), name="weight_grads",
        in_specs=[full(T, 256), full(T, 32), nat, nat, nat, nat, row(16), block,
                  pl.BlockSpec((2, 8, 32, 512), lambda i: (i, 0, 0, 0)), row(8), pl.BlockSpec((N, 8, 128), lambda i: (0, i, 0))],
        out_specs=[nat, block],
        out_shape=[S((T, E), jnp.float32), S((E // 512, 8, 80, 512), jnp.bfloat16)],
        scratch_shapes=[pltpu.VMEM((T, 384), jnp.bfloat16), pltpu.VMEM((T + 8, 1024), jnp.float32), pltpu.VMEM((384, 512), jnp.float32)],
        compiler_params=pltpu.CompilerParams(vmem_limit_bytes=48 * 2**20),
    )(glow, gbc, gcx, slope, xc, x, halo, wg, gdt, par, ga)


def input_grad_kernel(g_ref, edge_ref, cw_ref, out_ref, ext):
    last = lax.axis_index("seq") == 15
    ext[0:T, :] = g_ref[...]
    ext[T:T + 8, :] = jnp.where(last, 0.0, edge_ref[...])
    total = cw_ref[0:1, :] * ext[3:3 + T, :]
    for k in range(1, 4):
        total = total + cw_ref[k:k + 1, :] * ext[3 - k:3 - k + T, :]
    out_ref[...] = total.astype(jnp.bfloat16)


def input_grad(g_conv, edge, cw):
    E = g_conv.shape[1]
    nat, row, full = tile_specs(1024)
    return pl.pallas_call(
        input_grad_kernel, grid=(E // 1024,), name="input_grad",
        in_specs=[nat, row(8), row(4)], out_specs=nat,
        out_shape=jax.ShapeDtypeStruct((T, E), jnp.bfloat16),
        scratch_shapes=[pltpu.VMEM((T + 8, 1024), jnp.float32)],
        compiler_params=pltpu.CompilerParams(vmem_limit_bytes=48 * 2**20),
    )(g_conv, edge, cw)


def local(x_branch, z_branch, out_grad, x_weight, dt_weight, conv_weight, conv_bias, dt_bias, a_log, d_skip):
    x, z, g = x_branch[0], z_branch[0], out_grad[0]
    E = x.shape[1]
    shard = jnp.concatenate([x_weight.T, jnp.zeros((12, 512), jnp.bfloat16), dt_weight], axis=0)
    gathered, halo = gather(shard, x[T - 16:], tuple(zip(ORDERS, ROWS)), 0)
    wg = gathered.reshape(16, 8, 80, 512)
    a2_wide = -jnp.exp(a_log) * LOG2E
    a2 = a2_wide.reshape(N, E // 128, 128)
    a2_blocks = a2_wide.reshape(N, 16, 4, 128).transpose(1, 0, 2, 3).reshape(16, 64, 128)
    xc, slope, low, bc = conv_project(x, halo, conv_weight, conv_bias[None], wg)
    step3, drive3, gs3, sig, ends, tot = local_scan(low, wg, xc, z, g, dt_bias[None], a2, bc)
    carried = carry(ends, tot, a2_blocks)
    mixer_out, grad_z, gcx, gdt, par, ga, glow, gbc = main_scan(
        step3, drive3, gs3, sig, xc, z, g, d_skip[None], a2, bc, carried, wg, low
    )
    g_conv, part = weight_grads(glow, jnp.sum(gbc, axis=2), gcx, slope, xc, x, halo, wg, gdt, par, ga)
    reduced, params, edge = reduce_all(part.reshape(4, 4, 4, 2, 80, 512), g_conv[:8])
    grad_x = input_grad(g_conv, edge, conv_weight)
    params = params.reshape(16, 8, 16, 128)[:, :, :12].reshape(16, 8, 3, 4, 128)
    params = params.transpose(1, 2, 0, 3, 4).reshape(24, E).astype(jnp.float32)
    return (
        mixer_out[None], grad_x[None], grad_z[None], reduced[:36].T, reduced[48:80],
        params[0:4], params[4], params[5], params[7:23], params[6],
    )


def solution(mesh):
    tokens, weights, whole = P("dp", "seq", None), P("seq", "dp"), P()
    in_specs = (tokens,) * 3 + (weights, P("dp", "seq")) + (whole,) * 5
    out_specs = (tokens,) * 3 + (weights, P("dp", "seq")) + (whole,) * 5
    return jax.shard_map(local, mesh=mesh, in_specs=in_specs, out_specs=out_specs, check_vma=False)
```

time: 1800 us -> 377 us (0.21); the launches traced: 1780 us -> 377 us
  waiting for transfers between devices: 652 us -> 0 us
  other arithmetic: 583 us -> 4.92 us
  local copies, waits for them, and re-layouts: 431 us -> 21.2 us
  Pallas kernels: 0 us -> 350 us
  blocking collectives: 46.8 us -> 0 us
  matrix products: 33.4 us -> 0 us
    pallas_call x0 -> x8, Pallas kernels: none -> 350 us  [the longest x1 107 us: main_scan(): pl.pallas_call(main_scan_kernel, grid=(C,), name='main_scan', in_specs=[t...]
    reduce_sum x194 -> x1, other arithmetic: 291 us -> 2.21 us  [local(): jnp.sum(gbc, axis=2)]
    psum x2 -> x0, waiting for transfers between devices: 273 us -> none  [local(): lax.psum((grad_conv_w, grad_conv_b, grad_bias, grad_alog, grad_skip), ('d...]
    all_gather x5 -> x0, waiting for transfers between devices: 207 us -> none  [the longest x3 125 us: carried_in(): pieces = jax.tree.map(lambda part: lax.all_gather(part, axis), value)]
    reduce_scatter x3 -> x0, waiting for transfers between devices: 163 us -> none  [the longest x1 90.5 us: local(): lax.psum_scatter(g_wx_full, 'seq', scatter_dimension=0, tiled=True)]
    slice x71 -> x6, local copies, waits for them, and re-layouts: 167 us -> 5.49 us  [the longest x1 1.67 us: local(): gathered, halo = gather(shard, x[T - 16:], tuple(zip(ORDERS, ROWS)), 0)]
    another operation x2 -> x0, other arithmetic: 145 us -> none  [the longest x1 144 us: local(): cumul = jnp.cumsum(step_size, axis=0)]
    another operation x85 -> x0, local copies, waits for them, and re-layouts: 77.4 us -> none  [the longest x64 62.7 us: retreat(): jnp.stack(collected[::-1])]
  transfers between devices with their start and end apart: 13 -> 0, of which waited for: 12 -> 0; matrix products, arithmetic and copies ran while one was open for 9% -> 0% of each run, Pallas kernels for 0% -> 0%
where the time goes in v1:
time: 377 us
  Pallas kernels  350 us (93%)
  local copies, waits for them, and re-layouts  21.2 us (6%)
  other arithmetic  4.92 us (1%)
    pallas_call x1, Pallas kernels, main_scan(): pl.pallas_call(main_scan_kernel, grid=(C,), name='main_scan', in_specs=[t...  107 us
    pallas_call x1, Pallas kernels, reduce_all(): pl.pallas_call(reduce_kernel, name='reduce_shards', out_shape=[jax.ShapeD...  77 us
    pallas_call x1, Pallas kernels, local_scan(): pl.pallas_call(local_scan_kernel, grid=(C,), name='local_scan', in_specs=...  58.5 us
    pallas_call x1, Pallas kernels, gather(): pl.pallas_call(functools.partial(gather_kernel, parts, tail is not None),...  51.2 us
    pallas_call x1, Pallas kernels, carry(): pl.pallas_call(carry_kernel, name='carry_exchange', out_shape=jax.ShapeDt...  22.3 us
    pallas_call x1, Pallas kernels, weight_grads(): pl.pallas_call(grads_kernel, grid=(E // 1024,), name='weight_grads', in_s...  16 us
    unnamed x34, local copies, waits for them, and re-layouts  13.9 us
    pallas_call x1, Pallas kernels, conv_project(): pl.pallas_call(conv_kernel, grid=(E // 1024,), name='conv_project', in_sp...  12 us

profile of v1, /device:TPU:1, one launch (start us, length us, event | category | flops | bytes accessed | tf_op | source)
XLA Modules:
  0.0 376.6 jit_solution(15130885342009631965)
XLA Ops:
  0.6 0.0 copy-start.9
  0.7 0.0 copy-start.15
  0.7 0.1 pad.1.clone
  0.7 1.5 pad_maximum_fusion.refs_0_
  2.3 1.7 slice_bitcast_fusion.refs_1_
  3.9 1.1 negate_multiply_fusion
  5.1 0.4 reshape.47
  5.4 0.1 copy.24
  5.6 0.9 copy.28
  6.5 51.2 %gather_shards.1 = (bf16[4,4,4,2,80,512]{5,4,3,2,1,0:T(8,128)(2,1)}, bf16[16,8192]{1,0:T(8,128)(2,1)}) custom-call(bf16[80,512]{1,0:T(8,128)(2,1)} %pad_maximum_fusion.refs_0_, bf16[16,8192]{1,0:T(8,128)(2,1)} %slice_bitcast_fusion.refs_1_), custom_call_target="tpu_custom_call" | custom-call | tf_op jit(solution)/shard_map/gather_shards/pallas_call | solution.py:339
  57.6 0.0 copy-done.9
  57.6 0.0 copy-done.15
  57.7 0.0 copy-start.6
  57.7 0.9 copy-done.6
  58.6 12.0 %conv_project.1 = (bf16[128,8192]{1,0:T(8,128)(2,1)S(1)}, f32[128,8192]{1,0:T(8,128)}, bf16[128,256]{1,0:T(8,128)(2,1)S(1)}, f32[32,128,128]{2,1,0:T(8,128)S(1)}) custom-call(bf16[128,8192]{1,0:T(8,128)(2,1)} %bitcast.31, bf16[16,8192]{1,0:T(8,128)(2,1)S(1)} %copy-done.6, f32[4,8192]{1,0:T(4,128)S(1)} %copy-done.9, f32[1,8192]{1,0:T(1,128)S(1)} %bitcast.35, ...), custom_call_target="tpu_custom_call" | custom-call | tf_op jit(solution)/shard_map/conv_project/pallas_call | solution.py:650
  70.6 1.3 copy-done
  71.9 1.3 copy-done.3
  73.2 0.6 copy-done.12
  73.8 58.5 %local_scan.1 = (f32[128,64,128]{2,1,0:T(8,128)}, f32[128,64,128]{2,1,0:T(8,128)}, f32[128,64,128]{2,1,0:T(8,128)}, f32[128,8192]{1,0:T(8,128)}, bf16[16,128,128]{2,1,0:T(8,128)(2,1)}, /*index=5*/f32[16,8,128]{2,1,0:T(8,128)}) custom-call(bf16[128,256]{1,0:T(8,128)(2,1)} %copy-done.12, bf16[16,8,80,512]{3,2,1,0:T(8,128)(2,1)} %bitcast.37, ...), custom_call_target="tpu_custom_call" | custom-call | tf_op jit(solution)/shard_map/local_scan/pallas_call | solution.py:70
  132.3 0.0 copy-start.10
  132.3 1.0 copy-done.10
  133.3 0.8 copy-done.14
  134.2 22.3 %carry_exchange.1.ent_ref = bf16[16,128,128]{2,1,0:T(8,128)(2,1)S(1)} custom-call(bf16[16,128,128]{2,1,0:T(8,128)(2,1)S(1)} %copy-done.10, f32[16,8,128]{2,1,0:T(8,128)S(1)} %copy-done.14, f32[16,64,128]{2,1,0:T(8,128)S(1)} %bitcast.33), custom_call_target="tpu_custom_call" | custom-call | tf_op jit(solution)/shard_map/carry_exchange/pallas_call | solution.py:397
  156.5 0.0 copy-start.5
  156.6 0.8 copy-done.5
  157.3 107.0 %main_scan.1 = (bf16[128,8192]{1,0:T(8,128)(2,1)}, bf16[128,8192]{1,0:T(8,128)(2,1)}, f32[128,8192]{1,0:T(8,128)}, bf16[16,8,32,512]{3,2,1,0:T(8,128)(2,1)}, f32...) custom-call(f32[128,64,128]{2,1,0:T(8,128)} %get-tuple-element.40.step_ref, ...), custom_call_target="tpu_custom_call" | custom-call | tf_op jit(solution)/shard_map/main_scan/pallas_call | solution.py:186
  264.4 2.2 reduce_sum.9.gbc_ref
  266.6 0.0 copy-done.7
  266.6 0.0 copy-start.1
  266.6 1.6 copy-done.1
  268.2 1.6 copy-done.2
  269.8 1.0 copy-done.8
  270.8 0.9 copy-done.11
  271.8 0.9 copy-done.13
  272.7 16.0 %weight_grads.1 = (f32[128,8192]{1,0:T(8,128)}, bf16[16,8,80,512]{3,2,1,0:T(8,128)(2,1)}) custom-call(f32[128,256]{1,0:T(8,128)S(1)} %copy-done.13, f32[128,32]{1,0:T(8,128)S(1)} %reduce_sum.9.gbc_ref, f32[128,8192]{1,0:T(8,128)} %get-tuple-element.49.gcx_ref, f32[128,8192]{1,0:T(8,128)} %get-tuple-element.50.slope_ref, bf16[128,8192]{1,0:T(8,128)(2,1)S(1)} %copy-done.1, ...), custom_call_target="tpu_custom_call" | custom-call | tf_op jit(solution)/shard_map/weight_grads/pallas_call | solution.py:700
  288.7 1.0 slice.35.edge
  289.6 0.0 copy-start.4
  289.7 77.0 %reduce_shards.1 = (f32[80,512]{1,0:T(8,128)S(1)}, bf16[4,4,4,2,16,128]{5,4,3,2,1,0:T(8,128)(2,1)S(1)}, f32[8,8192]{1,0:T(8,128)S(1)}) custom-call(bf16[4,4,4,2,80,512]{5,4,3,2,1,0:T(8,128)(2,1)} %bitcast.40, f32[8,8192]{1,0:T(8,128)S(1)} %slice.35.edge), custom_call_target="tpu_custom_call" | custom-call | tf_op jit(solution)/shard_map/reduce_shards/pallas_call | solution.py:578
  366.7 5.6 %input_grad.1 = bf16[128,8192]{1,0:T(8,128)(2,1)} custom-call(f32[128,8192]{1,0:T(8,128)S(1)} %copy-done.4, f32[8,8192]{1,0:T(8,128)S(1)} %get-tuple-element.56.edge_ref, f32[4,8192]{1,0:T(4,128)S(1)} %copy-done.9), custom_call_target="tpu_custom_call" | custom-call | tf_op jit(solution)/shard_map/input_grad/pallas_call | solution.py:724
  372.4 0.1 copy.27
  372.5 0.6 slice.37
  373.1 0.6 slice_bitcast_fusion.1
  373.7 0.1 convert_bitcast_fusion
  373.8 0.2 copy.26
  374.0 0.3 reshape.51
  374.4 0.7 fusion.1
  375.1 0.7 slice.45
  375.8 0.8 slice.48
  (11 shorter events, 0.0 us)
Async XLA Ops:
  0.6 57.0 %copy-start.9 = (f32[4,8192]{1,0:T(4,128)S(1)}, f32[4,8192]{1,0:T(4,128)}, u32[]{:S(2)}) copy-start(f32[4,8192]{1,0:T(4,128)} %cw_ref.3) | copy-start | bytes 393220
  0.7 57.0 %copy-start.15 = (f32[8192]{0:T(1024)S(1)}, f32[8192]{0:T(1024)}, u32[]{:S(2)}) copy-start(f32[8192]{0:T(1024)} %param.16) | copy-start | bytes 98308
  57.7 1.0 copy-start.6
  70.6 1.3 copy-start
  71.9 1.3 copy-start.3
  73.2 0.6 copy-start.12
  132.3 1.0 copy-start.10
  133.3 0.8 copy-start.14
  156.5 0.8 copy-start.5
  157.3 109.2 %copy-start.7 = (bf16[16,8192]{1,0:T(8,128)(2,1)S(1)}, bf16[16,8192]{1,0:T(8,128)(2,1)}, u32[]{:S(2)}) copy-start(bf16[16,8192]{1,0:T(8,128)(2,1)} %get-tuple-element.35.halo_ref) | copy-start | bytes 786436
  266.6 1.6 copy-start.1
  268.2 1.6 copy-start.2
  269.8 1.0 copy-start.8
  270.8 0.9 copy-start.11
  271.8 0.9 copy-start.13
  289.6 77.1 %copy-start.4 = (f32[128,8192]{1,0:T(8,128)S(1)}, f32[128,8192]{1,0:T(8,128)}, u32[]{:S(2)}) copy-start(f32[128,8192]{1,0:T(8,128)} %get-tuple-element.54.g_ref) | copy-start | bytes 12582916

commit v2 on v1

v2 whole, which is shorter than its diff:
```python
import functools

import jax
import jax.numpy as jnp
from jax import lax
from jax.experimental import pallas as pl
from jax.experimental.pallas import tpu as pltpu
from jax.sharding import PartitionSpec as P

T = 128
N = 16
LN2 = 0.6931471805599453
LOG2E = 1.4426950408889634
VMEM_LIMIT = 62 * 2**20
LOCAL_GROUP, LOCAL_UNROLL = 4, 16
CHUNKS = 1
FWD_GROUP, FWD_UNROLL = 8, 8
BWD_GROUP, BWD_UNROLL = 8, 8


def logistic(values):
    return 0.5 * jnp.tanh(0.5 * values) + 0.5


def tile_specs(width):
    nat = pl.BlockSpec((T, width), lambda i: (0, i))
    row = lambda count: pl.BlockSpec((count, width), lambda i: (0, i))
    full = lambda *shape: pl.BlockSpec(shape, lambda i: (0,) * len(shape))
    return nat, row, full


def local_scan_kernel(low_ref, wa_ref, wb_ref, x_ref, z_ref, g_ref, bias_ref, a2_ref, bc_ref,
                      step_ref, drive_ref, gs_ref, sig_ref, ends_ref, tot_ref, scr):
    low = low_ref[...]
    rows = [ref.reshape(T * 8, 128) for ref in (step_ref, drive_ref, gs_ref)]
    for half in range(2):
        dt = jnp.concatenate([wa_ref[half].reshape(128, 512), wb_ref[half].reshape(128, 512)], axis=0)
        cols = pl.ds(512 * half, 512)
        rate = jnp.dot(low, dt, preferred_element_type=jnp.float32) + bias_ref[:, cols]
        step = jnp.maximum(rate, 0.0) + jnp.log1p(jnp.exp(-jnp.abs(rate)))
        sig_ref[:, cols] = jnp.exp(rate - step)
        z = z_ref[:, cols].astype(jnp.float32)
        gs = g_ref[:, cols].astype(jnp.float32) * (z * logistic(z))
        drive = step * x_ref[:, cols].astype(jnp.float32)
        for s in range(4):
            for ref, value in zip(rows, (step, drive, gs)):
                ref[pl.ds(4 * half + s, T, stride=8), :] = value[:, 128 * s:128 * s + 128]

    zero = jnp.zeros((8, 128), jnp.float32)
    one = jnp.ones((8, 128), jnp.float32)
    ends, lams = [], []
    for first in range(0, N, LOCAL_GROUP):
        group = range(first, first + LOCAL_GROUP)

        def body(k, carry):
            tot, ends, prods, lams = carry
            for unrolled in range(LOCAL_UNROLL):
                t = k * LOCAL_UNROLL + unrolled
                st, dr, gv = step_ref[t], drive_ref[t], gs_ref[t]
                new_ends, new_prods, new_lams = [], [], []
                for q, n in enumerate(group):
                    f = jnp.exp2(st * a2_ref[n])
                    new_ends.append(f * ends[q] + bc_ref[n, pl.ds(t, 1), :] * dr)
                    p = prods[q] * f
                    new_prods.append(p)
                    new_lams.append(lams[q] + p * (bc_ref[N + n, pl.ds(t, 1), :] * gv))
                tot, ends, prods, lams = tot + st, tuple(new_ends), tuple(new_prods), tuple(new_lams)
            return tot, ends, prods, lams

        many = LOCAL_GROUP
        tot, e, _, l = lax.fori_loop(0, T // LOCAL_UNROLL, body, (zero, (zero,) * many, (one,) * many, (zero,) * many))
        ends += e
        lams += l
    for n in range(N):
        for half in range(2):
            scr[half, 4 * n:4 * n + 4, :] = ends[n][4 * half:4 * half + 4]
            scr[half, 64 + 4 * n:64 + 4 * n + 4, :] = lams[n][4 * half:4 * half + 4]
    ends_ref[...] = scr[...].astype(jnp.bfloat16)
    for half in range(2):
        tot_ref[half, 0:4, :] = tot[4 * half:4 * half + 4]
        tot_ref[half, 4:8, :] = jnp.zeros((4, 128), jnp.float32)


def local_scan(low, wg, x_conv, z, g, bias, a2, bc):
    E = x_conv.shape[1]
    C = E // 1024
    f32 = jnp.float32
    nat, row, full = tile_specs(1024)
    tri = pl.BlockSpec((T, 8, 128), lambda i: (0, i, 0))
    return pl.pallas_call(
        local_scan_kernel, grid=(C,), name="local_scan",
        in_specs=[full(T, 256), pl.BlockSpec((2, 8, 16, 512), lambda i: (i, 0, 3, 0)),
                  pl.BlockSpec((2, 8, 16, 512), lambda i: (i, 0, 4, 0)), nat, nat, nat,
                  row(1), pl.BlockSpec((N, 8, 128), lambda i: (0, i, 0)), full(32, T, 128)],
        out_specs=[tri, tri, tri, nat, pl.BlockSpec((2, 128, 128), lambda i: (i, 0, 0)),
                   pl.BlockSpec((2, 8, 128), lambda i: (i, 0, 0))],
        out_shape=[jax.ShapeDtypeStruct((T, E // 128, 128), f32)] * 3 + [
            jax.ShapeDtypeStruct((T, E), f32), jax.ShapeDtypeStruct((2 * C, 128, 128), jnp.bfloat16),
            jax.ShapeDtypeStruct((2 * C, 8, 128), f32)],
        scratch_shapes=[pltpu.VMEM((2, 128, 128), f32)],
        compiler_params=pltpu.CompilerParams(vmem_limit_bytes=VMEM_LIMIT),
    )(low, wg, wg, x_conv, z, g, bias, a2, bc)


def main_scan_kernel(step_ref, drive_ref, gs_ref, sig_ref, x_ref, z_ref, g_ref, dskip_ref, a2_ref, bc_ref, ent_ref, wa_ref, wb_ref, low_ref,
              mix_ref, gz_ref, gcx_ref, gdt_ref, par_ref, ga_ref, glow_ref, gbc_ref,
              es, us, y3, gd3, gr3, accb, accc, alow, turned):
    i = pl.program_id(0)
    f32 = jnp.float32
    span = [slice(8 * q, 8 * q + 8) for q in range(CHUNKS)]

    @pl.when(i == 0)
    def _():
        accb[...] = jnp.zeros(accb.shape, f32)
        accc[...] = jnp.zeros(accc.shape, f32)
        alow[...] = jnp.zeros(alow.shape, f32)
        turned[...] = low_ref[...].T

    es[...] = ent_ref[...].astype(f32)

    def state(base, n, q):
        rows = slice(base + 4 * n, base + 4 * n + 4)
        return jnp.concatenate([es[2 * q, rows, :], es[2 * q + 1, rows, :]], axis=0)

    def add(total, term):
        return term if total is None else total + term

    def inputs(t):
        return tuple([ref[t, rows] for rows in span] for ref in (step_ref, drive_ref, gs_ref))

    zero = jnp.zeros((8, 128), f32)
    for first in range(0, N, FWD_GROUP):
        group = range(first, first + FWD_GROUP)

        def forward(k, hs):
            for unrolled in range(FWD_UNROLL):
                t = k * FWD_UNROLL + unrolled
                st, dr, gv = inputs(t)
                ys = [None if first == 0 else y3[t, rows] for rows in span]
                new = []
                for p, n in enumerate(group):
                    b, c = bc_ref[n, pl.ds(t, 1), :], bc_ref[N + n, pl.ds(t, 1), :]
                    total = accc[t, n]
                    for q in range(CHUNKS):
                        u = jnp.exp2(st[q] * a2_ref[n, span[q]]) * hs[p * CHUNKS + q]
                        us[t, n, span[q]] = u
                        h = u + b * dr[q]
                        new.append(h)
                        ys[q] = add(ys[q], c * h)
                        total = total + h * gv[q]
                    accc[t, n] = total
                for q in range(CHUNKS):
                    y3[t, span[q]] = ys[q]
                hs = tuple(new)
            return hs

        lax.fori_loop(0, T // FWD_UNROLL, forward, tuple(state(0, n, q) for n in group for q in range(CHUNKS)))

    for first in range(0, N, BWD_GROUP):
        group = range(first, first + BWD_GROUP)

        def backward(k, carry):
            adj, ra = carry
            for unrolled in range(BWD_UNROLL):
                t = T - 1 - (k * BWD_UNROLL + unrolled)
                st, dr, gv = inputs(t)
                gd = [None if first == 0 else gd3[t, rows] for rows in span]
                gr = [None if first == 0 else gr3[t, rows] for rows in span]
                na, nr = [], []
                for p, n in enumerate(group):
                    b, c = bc_ref[n, pl.ds(t, 1), :], bc_ref[N + n, pl.ds(t, 1), :]
                    total = accb[t, n]
                    for q in range(CHUNKS):
                        rate = a2_ref[n, span[q]]
                        lam = c * gv[q] + adj[p * CHUNKS + q]
                        gd[q] = add(gd[q], lam * b)
                        total = total + lam * dr[q]
                        na.append(jnp.exp2(st[q] * rate) * lam)
                        m = lam * us[t, n, span[q]]
                        gr[q] = add(gr[q], m * rate)
                        nr.append(ra[p * CHUNKS + q] + m * st[q])
                    accb[t, n] = total
                for q in range(CHUNKS):
                    gd3[t, span[q]] = gd[q]
                    gr3[t, span[q]] = gr[q]
                adj, ra = tuple(na), tuple(nr)
            return adj, ra

        _, ra = lax.fori_loop(0, T // BWD_UNROLL, backward, (tuple(state(64, n, q) for n in group for q in range(CHUNKS)), (zero,) * (BWD_GROUP * CHUNKS)))
        for p, n in enumerate(group):
            for q in range(CHUNKS):
                ga_ref[n, span[q]] = ra[p * CHUNKS + q] * a2_ref[n, span[q]] * LN2

    for half in range(2 * CHUNKS):
        dt = jnp.concatenate([wa_ref[half].reshape(128, 512), wb_ref[half].reshape(128, 512)], axis=0)
        gpb = []
        for s in range(4 * half, 4 * half + 4):
            cols = slice(128 * s, 128 * s + 128)
            xw = x_ref[:, cols].astype(f32)
            z = z_ref[:, cols].astype(f32)
            gw = g_ref[:, cols].astype(f32)
            dsk = dskip_ref[:, cols]
            sz = logistic(z)
            act = z * sz
            inner = y3.reshape(T * 8 * CHUNKS, 128)[pl.ds(s, T, stride=8 * CHUNKS), :] + dsk * xw
            mix_ref[:, cols] = (act * inner).astype(jnp.bfloat16)
            gz_ref[:, cols] = (gw * inner * (sz + act * (1.0 - sz))).astype(jnp.bfloat16)
            gsn = gw * act
            gd = gd3.reshape(T * 8 * CHUNKS, 128)[pl.ds(s, T, stride=8 * CHUNKS), :]
            gpre = (gd * xw + gr3.reshape(T * 8 * CHUNKS, 128)[pl.ds(s, T, stride=8 * CHUNKS), :] * LN2) * sig_ref[:, cols]
            gcx_ref[:, cols] = gd * step_ref.reshape(T * 8 * CHUNKS, 128)[pl.ds(s, T, stride=8 * CHUNKS), :] + gsn * dsk
            par_ref[0:1, cols] = jnp.sum(gpre, axis=0, keepdims=True)
            par_ref[1:2, cols] = jnp.sum(gsn * xw, axis=0, keepdims=True)
            gpb.append(gpre.astype(jnp.bfloat16))
        gp = jnp.concatenate(gpb, axis=1)
        alow[...] += lax.dot_general(gp, dt, (((1,), (1,)), ((), ())), preferred_element_type=f32)
        gdt = jnp.dot(turned[...], gp, preferred_element_type=f32).astype(jnp.bfloat16)
        for h in range(2):
            gdt_ref[half, :, 16 * h:16 * h + 16, :] = gdt[128 * h:128 * h + 128].reshape(8, 16, 512)

    @pl.when(i == pl.num_programs(0) - 1)
    def _():
        glow_ref[...] = alow[...]

        def fold(t, _):
            gbc_ref[t, 0:16, :] = jnp.sum(accb[t], axis=1)
            gbc_ref[t, 16:32, :] = jnp.sum(accc[t], axis=1)
            return 0
        lax.fori_loop(0, T, fold, 0)

def main_scan(step3, drive3, gs3, sig, x_conv, z, g, dskip, a2, bc, ent, wg, low):
    E = x_conv.shape[1]
    C = E // (1024 * CHUNKS)
    f32 = jnp.float32
    nat = pl.BlockSpec((T, 1024 * CHUNKS), lambda i: (0, i))
    tri = pl.BlockSpec((T, 8 * CHUNKS, 128), lambda i: (0, i, 0))
    row = lambda count: pl.BlockSpec((count, 1024 * CHUNKS), lambda i: (0, i))
    once = lambda *shape: pl.BlockSpec(shape, lambda i: (0,) * len(shape), pipeline_mode=pl.Buffered(1))
    full = lambda *shape: pl.BlockSpec(shape, lambda i: (0,) * len(shape))
    rate = pl.BlockSpec((N, 8 * CHUNKS, 128), lambda i: (0, i, 0))
    S = jax.ShapeDtypeStruct
    return pl.pallas_call(
        main_scan_kernel, grid=(C,), name="main_scan",
        in_specs=[tri, tri, tri, nat, nat, nat, nat, row(1), rate, once(32, T, 128),
                  pl.BlockSpec((2 * CHUNKS, 128, 128), lambda i: (i, 0, 0)),
                  pl.BlockSpec((2 * CHUNKS, 8, 16, 512), lambda i: (i, 0, 3, 0)),
                  pl.BlockSpec((2 * CHUNKS, 8, 16, 512), lambda i: (i, 0, 4, 0)), once(T, 256)],
        out_specs=[nat, nat, nat, pl.BlockSpec((2 * CHUNKS, 8, 32, 512), lambda i: (i, 0, 0, 0)),
                   row(8), rate, full(T, 256), full(T, 32, 128)],
        out_shape=[S((T, E), jnp.bfloat16), S((T, E), jnp.bfloat16), S((T, E), f32), S((E // 512, 8, 32, 512), jnp.bfloat16),
                   S((8, E), f32), S((N, E // 128, 128), f32), S((T, 256), f32), S((T, 32, 128), f32)],
        scratch_shapes=[pltpu.VMEM((2 * CHUNKS, 128, 128), f32), pltpu.VMEM((T, N, 8 * CHUNKS, 128), f32)]
        + [pltpu.VMEM((T, 8 * CHUNKS, 128), f32)] * 3 + [pltpu.VMEM((T, N, 8, 128), f32)] * 2 + [pltpu.VMEM((T, 256), f32), pltpu.VMEM((256, T), jnp.bfloat16)],
        compiler_params=pltpu.CompilerParams(vmem_limit_bytes=VMEM_LIMIT),
    )(step3, drive3, gs3, sig, x_conv, z, g, dskip, a2, bc, ent, wg, wg, low)


MESH = pl.DeviceIdType.MESH
ORDERS = (("x", "y", "z"), ("y", "z", "x"), ("z", "x", "y"))
GATHER_ROWS = ((0, 32), (32, 32), (64, 16))
ROWS = ((0, 32), (32, 16), (48, 32))
DIMS = {"z": 0, "x": 1, "y": 2}


def place():
    d, j = lax.axis_index("dp"), lax.axis_index("seq")
    return d, j, {"z": lax.div(j, 4), "x": lax.rem(j, 4), "y": lax.div(d, 2)}, lax.rem(d, 2)


def peer(pos, core, axis, hop):
    at = dict(pos)
    at[axis] = lax.rem(at[axis] + hop + 4, 4)
    return (at["y"] * 2 + core, at["z"] * 4 + at["x"])


OTHERS = [(a, b) for a in range(4) for b in range(4) if (a, b) != (0, 0)]


def peer2(pos, core, axes, hops):
    at = {a: lax.rem(pos[a] + h, 4) for a, h in zip(axes, hops)}
    at = {**pos, **at}
    return (at["y"] * 2 + core, at["z"] * 4 + at["x"])


def planes(pos, core):
    near = [peer(pos, core, axis, hop) for axis in "xyz" for hop in (1, 2, 3)]
    return near + [peer2(pos, core, axes, (a, b)) for axes in ("xy", "yz", "zx") for a, b in OTHERS if a and b]


def greet(devices):
    barrier = pltpu.get_barrier_semaphore()
    for device in devices:
        pl.semaphore_signal(barrier, inc=1, device_id=device, device_id_type=MESH)
    pl.semaphore_wait(barrier, len(devices))


def remote(src, dst, send_sem, recv_sem, device):
    return pltpu.make_async_remote_copy(
        src_ref=src, dst_ref=dst, send_sem=send_sem, recv_sem=recv_sem, device_id=device, device_id_type=MESH
    )


def slab(ref, fixed, tail):
    index = [slice(None)] * 3
    for axis, value in fixed.items():
        index[DIMS[axis]] = value
    return ref.at[tuple(index) + tail]


def gather_kernel(parts, with_tail, *refs):
    if with_tail:
        shard, tail_ref, out, halo, local_sem, ssem, rsem, fsend, frecv, csend, crecv, hsend, hrecv = refs
    else:
        shard, out, local_sem, ssem, rsem, fsend, frecv, csend, crecv = refs
    d, j, pos, core = place()
    sibling = (pos["y"] * 2 + 1 - core, j)
    following, previous = (d, lax.rem(j + 1, 16)), (d, lax.rem(j + 15, 16))
    greet(planes(pos, core) + [sibling] + ([previous] if with_tail else []))
    sent = []

    def go(copy):
        copy.start()
        sent.append(copy)

    own = out.at[pos["z"], pos["x"], pos["y"], core]
    local = pltpu.make_async_copy(shard, own, local_sem)
    local.start()
    half = out.shape[-1] // 2
    columns = (pl.ds(0, half), pl.ds(half, half))
    whole = slice(None)
    hops = (0, -1, 1, 2)

    def step(p, slot, axis, fixed):
        row, count = parts[p][1]
        rows = pl.ds(row, count)
        right, left = peer(pos, core, axis, 1), peer(pos, core, axis, -1)

        def at(hop, cols=whole, which=core):
            return slab(out, {**fixed, axis: lax.rem(pos[axis] + hop + 4, 4)}, (which, rows, cols))

        def ring(hop, cols, which, device):
            return remote(at(hop, cols), at(hop, cols), ssem.at[p, slot, which], rsem.at[p, slot, which], device)

        def send(which):
            hop, cols, device = ((0, whole, right), (0, whole, left), (-1, columns[0], right), (1, columns[1], left))[which]
            go(ring(hop, cols, which, device))

        def landed(which):
            hop, cols, device = ((-1, whole, right), (1, whole, left), (2, columns[0], right), (2, columns[1], left))[which]
            ring(hop, cols, which, device).wait_recv()

        def across(which):
            there = at(hops[which])
            go(remote(there, there, csend.at[p, slot, which], crecv.at[p, slot, which], sibling))

        def crossed(which):
            there = at(hops[which], whole, 1 - core)
            remote(there, there, csend.at[p, slot, which], crecv.at[p, slot, which], sibling).wait_recv()

        return send, landed, across, crossed

    count = range(len(parts))

    def spot(axis, hop):
        return lax.rem(pos[axis] + hop + 4, 4)

    def direct(p, k):
        (one, two, three), (row, rows) = parts[p]
        device = peer2(pos, core, (one, two), OTHERS[k])
        return remote(shard.at[pl.ds(row, rows), :], own.at[pl.ds(row, rows), :], fsend.at[p, k], frecv.at[p, k], device)

    def arrived(p, k):
        (one, two, three), (row, rows) = parts[p]
        a, b = OTHERS[k]
        there = slab(out, {one: spot(one, -a), two: spot(two, -b), three: pos[three]}, (core, pl.ds(row, rows), whole))
        remote(there, there, fsend.at[p, k], frecv.at[p, k], peer2(pos, core, (one, two), OTHERS[k])).wait_recv()

    third = []
    for p in count:
        one, two, three = parts[p][0]
        third.append([step(p, i, three, {two: spot(two, hops[i])}) for i in range(4)])
    turn = [[k for k, (a, b) in enumerate(OTHERS) if (-b) % 4 == hops[i] % 4] for i in range(4)]
    for i in range(4):
        for k in turn[i]:
            for p in count:
                go(direct(p, k))
    if with_tail:
        tail_copy = remote(tail_ref.at[pl.ds(T - 16, 16), :], halo, hsend, hrecv, following)
        go(tail_copy)
    local.wait()
    for i in range(4):
        for p in count:
            for k in turn[i]:
                arrived(p, k)
            send, _, across, _ = third[p][i]
            send(0)
            send(1)
            across(0)
    for i in range(4):
        for which in (0, 1):
            for p in count:
                send, landed, across, _ = third[p][i]
                landed(which)
                send(2 + which)
                across(1 + which)
    for i in range(4):
        for p in count:
            _, landed, across, _ = third[p][i]
            landed(2)
            landed(3)
            across(3)
    for i in range(4):
        for p in count:
            for which in range(4):
                third[p][i][3](which)
    if with_tail:
        tail_copy.wait_recv()
    for copy in sent:
        copy.wait_send()


def gather(shard, tail, parts, collective_id):
    rows, columns = shard.shape
    count = len(parts)
    anyspace = pl.BlockSpec(memory_space=pl.ANY)
    dma = pltpu.SemaphoreType.DMA
    out_shape = [jax.ShapeDtypeStruct((4, 4, 4, 2, rows, columns), shard.dtype)]
    sems = [dma, dma((count, 4, 4)), dma((count, 4, 4)), dma((count, 15)), dma((count, 15)), dma((count, 4, 4)), dma((count, 4, 4))]
    operands = [shard]
    if tail is not None:
        out_shape.append(jax.ShapeDtypeStruct((16, tail.shape[1]), tail.dtype))
        sems += [dma, dma]
        operands.append(tail)
    return pl.pallas_call(
        functools.partial(gather_kernel, parts, tail is not None),
        name="gather_shards",
        out_shape=out_shape,
        in_specs=[anyspace] * len(operands),
        out_specs=[anyspace] * len(out_shape),
        scratch_shapes=sems,
        compiler_params=pltpu.CompilerParams(collective_id=collective_id, has_side_effects=True, vmem_limit_bytes=VMEM_LIMIT),
    )(*operands)


def carry_kernel(ends, tot, a2, out, got, got_tot, back, ssem, rsem, tsend, trecv, bsend, brecv):
    d, j, pos, core = place()
    peers = [(d, lax.rem(j + k, 16)) for k in range(1, 16)]
    greet(peers)
    sent = []
    for k in range(1, 16):
        to = lax.rem(j + k, 16)
        one = remote(ends.at[to], got.at[j], ssem.at[k], rsem.at[k], peers[k - 1])
        two = remote(tot.at[to], got_tot.at[j], tsend.at[k], trecv.at[k], peers[k - 1])
        one.start()
        two.start()
        sent += [one, two]
    got[j] = ends[j]
    got_tot[j] = tot[j]
    for k in range(1, 16):
        source = lax.rem(j + 16 - k, 16)
        remote(got.at[source], got.at[source], ssem.at[k], rsem.at[k], peers[k - 1]).wait_recv()
        remote(got_tot.at[source], got_tot.at[source], tsend.at[k], trecv.at[k], peers[k - 1]).wait_recv()
    rates = a2[j]

    def decay(i):
        return jnp.exp2(rates * jnp.concatenate([got_tot[i, 0:4, :]] * 16, axis=0))

    enter = jnp.zeros((64, 128), jnp.float32)
    leave = jnp.zeros((64, 128), jnp.float32)
    for i in range(16):
        back[i, 0:64, :] = enter.astype(jnp.bfloat16)
        enter = decay(i) * enter + got[i, 0:64, :].astype(jnp.float32)
        r = 15 - i
        back[r, 64:128, :] = leave.astype(jnp.bfloat16)
        leave = decay(r) * leave + got[r, 64:128, :].astype(jnp.float32)
    for k in range(1, 16):
        to = lax.rem(j + k, 16)
        one = remote(back.at[to], out.at[j], bsend.at[k], brecv.at[k], peers[k - 1])
        one.start()
        sent.append(one)
    out[j] = back[j]
    for k in range(1, 16):
        source = lax.rem(j + 16 - k, 16)
        remote(out.at[source], out.at[source], bsend.at[k], brecv.at[k], peers[k - 1]).wait_recv()
    for copy in sent:
        copy.wait_send()


def carry(ends, tot, a2):
    vmem = pl.BlockSpec(memory_space=pltpu.VMEM)
    dma = pltpu.SemaphoreType.DMA((16,))
    return pl.pallas_call(
        carry_kernel,
        name="carry_exchange",
        out_shape=jax.ShapeDtypeStruct((16, 128, 128), jnp.bfloat16),
        in_specs=[vmem] * 3,
        out_specs=vmem,
        scratch_shapes=[
            pltpu.VMEM((16, 128, 128), jnp.bfloat16),
            pltpu.VMEM((16, 8, 128), jnp.float32),
            pltpu.VMEM((16, 128, 128), jnp.bfloat16),
            dma, dma, dma, dma, dma, dma,
        ],
        compiler_params=pltpu.CompilerParams(
            collective_id=1, has_side_effects=True, vmem_limit_bytes=VMEM_LIMIT
        ),
    )(ends, tot, a2)


def reduce_kernel(xpart, dpart, edge, out, all_params, halo, sums, cross, *scratch):
    buffers, plane, scratch = scratch[:48], scratch[48:51], scratch[51:]
    packed, own_sem, csend, crecv, ssem, rsem, fsend, frecv, psend, precv, qsend, qrecv, hsend, hrecv = scratch
    d, j, pos, core = place()
    sibling = (pos["y"] * 2 + 1 - core, j)
    following, previous = (d, lax.rem(j + 1, 16)), (d, lax.rem(j + 15, 16))
    column = [(lax.rem(pos["y"] + k // 2, 4) * 2 + lax.rem(core + k, 2), j) for k in range(1, 8)]
    greet(planes(pos, core) + column + [following])
    sent = []
    hops = (2, 1, -1, 0)
    half = 256
    whole = slice(None)
    columns = (slice(0, half), slice(half, 2 * half))

    def go(copy):
        copy.start()
        sent.append(copy)

    def spot(axis, hop):
        return lax.rem(pos[axis] + hop + 4, 4)

    def mine(p, i, which):
        row, count = ROWS[p]
        fixed = {ORDERS[p][1]: spot(ORDERS[p][1], hops[i])}
        return slab(xpart if p < 2 else dpart, fixed, (which, pl.ds(row if p < 2 else 0, count), whole))

    def beside(ref, p, i):
        row, count = ROWS[p]
        return slab(ref, {ORDERS[p][1]: spot(ORDERS[p][1], hops[i])}, (pl.ds(row, count), whole))

    def across(p, i):
        return remote(mine(p, i, 1 - core), beside(cross, p, i), csend.at[p, i], crecv.at[p, i], sibling)

    def own(p, i):
        return pltpu.make_async_copy(mine(p, i, core), beside(sums, p, i), own_sem.at[p, i])

    for i in range(4):
        for p in range(3):
            go(across(p, i))
            own(p, i).start()
    edge_copy = remote(edge, halo, hsend, hrecv, previous)
    go(edge_copy)

    def index_of(fixed, free, values):
        index = [None] * 3
        for a, v in {**fixed, **dict(zip(free, values))}.items():
            index[DIMS[a]] = v
        return tuple(index)

    def add_core(p, i):
        row, count = ROWS[p]
        rows = pl.ds(row, count)
        middle = ORDERS[p][1]
        free = [a for a in "zxy" if a != middle]
        own(p, i).wait()
        across(p, i).wait_recv()

        def one(k, _):
            at = index_of({middle: spot(middle, hops[i])}, free, (lax.div(k, 4), lax.rem(k, 4))) + (rows, whole)
            sums[at] = (sums[at].astype(jnp.float32) + cross[at].astype(jnp.float32)).astype(jnp.bfloat16)
            return 0

        lax.fori_loop(0, 16, one, 0)

    def step(p, slot, axis, fixed, free):
        row, count = ROWS[p]
        rows = pl.ds(row, count)
        right, left = peer(pos, core, axis, 1), peer(pos, core, axis, -1)
        bufs = buffers[(p * 4 + slot) * 4:(p * 4 + slot) * 4 + 4]

        def copy(which):
            hop, cols, device = ((2, columns[0], right), (2, columns[1], left), (1, whole, right), (-1, whole, left))[which]
            source = slab(sums, {**fixed, axis: spot(axis, hop)}, (rows, cols))
            return remote(source, bufs[which], ssem.at[p, slot, which], rsem.at[p, slot, which], device)

        def add(hop, cols, terms):
            def one(k, _):
                at = index_of({**fixed, axis: spot(axis, hop)}, free, (k,)) + (rows, cols)
                total = sums[at].astype(jnp.float32)
                for term in terms:
                    total = total + term[k].astype(jnp.float32)
                sums[at] = total.astype(jnp.bfloat16)
                return 0

            lax.fori_loop(0, 4, one, 0)

        def begin():
            go(copy(0))
            go(copy(1))

        def relay(which):
            copy(which).wait_recv()
            add((1, -1)[which], columns[which], bufs[which:which + 1])
            go(copy(2 + which))

        def finish():
            copy(2).wait_recv()
            copy(3).wait_recv()
            add(0, whole, bufs[2:])

        return begin, relay, finish

    def direct(p, k):
        one, two, three = ORDERS[p]
        a, b = OTHERS[k]
        row, count = ROWS[p]
        source = slab(sums, {one: spot(one, a), two: spot(two, b), three: pos[three]}, (pl.ds(row, count), whole))
        return remote(source, plane[p].at[k], fsend.at[p, k], frecv.at[p, k], peer2(pos, core, (one, two), (a, b)))

    parts = range(3)
    turn = [[k for k, (a, b) in enumerate(OTHERS) if b % 4 == hops[i] % 4] for i in range(4)]
    outer = []
    for p in parts:
        one, two, three = ORDERS[p]
        outer.append([step(p, i, three, {two: spot(two, hops[i])}, [one]) for i in range(4)])
    for i in range(4):
        for p in parts:
            add_core(p, i)
            outer[p][i][0]()
    for i in range(4):
        for which in (0, 1):
            for p in parts:
                outer[p][i][1](which)
    for i in range(4):
        for p in parts:
            outer[p][i][2]()
            for k in turn[i]:
                go(direct(p, k))
    for p in parts:
        row, count = ROWS[p]
        rows = pl.ds(row, count)
        for k in range(15):
            direct(p, k).wait_recv()
        out[rows, :] = sums[pos["z"], pos["x"], pos["y"], rows, :].astype(jnp.float32)

        def one_more(k, _):
            out[rows, :] += plane[p][k].astype(jnp.float32)
            return 0

        lax.fori_loop(0, 15, one_more, 0)

    packed[...] = jnp.zeros((16, 128), jnp.bfloat16)
    rowsum = jnp.concatenate(
        [out[36 + q:37 + q, 128 * s:128 * s + 128] for q in range(3) for s in range(4)] + [jnp.zeros((4, 128), jnp.float32)], axis=0
    )
    packed[...] = rowsum.astype(jnp.bfloat16)
    all_params[pos["z"], pos["x"], pos["y"], core] = packed[...]

    def place_of(hops):
        return all_params.at[lax.rem(pos["z"] + 4 - hops[0], 4), lax.rem(pos["x"] + 4 - hops[1], 4), pos["y"], core]

    def flat(k):
        return remote(place_of((0, 0)), place_of((0, 0)), psend.at[k], precv.at[k], peer2(pos, core, "zx", OTHERS[k]))

    def upright(k):
        ours = all_params.at[:, :, pos["y"], core]
        return remote(ours, ours, qsend.at[k], qrecv.at[k], column[k - 1])

    for k in range(15):
        go(flat(k))
    for k in range(15):
        there = place_of(OTHERS[k])
        remote(there, there, psend.at[k], precv.at[k], peer2(pos, core, "zx", OTHERS[k])).wait_recv()
    for k in range(1, 8):
        go(upright(k))
    for k in range(1, 8):
        y, c = lax.rem(pos["y"] + 4 - k // 2, 4), lax.rem(core + k, 2)
        there = all_params.at[:, :, y, c]
        remote(there, there, qsend.at[k], qrecv.at[k], column[k - 1]).wait_recv()
    edge_copy.wait_recv()
    for copy in sent:
        copy.wait_send()


def reduce_all(xpart, dpart, edge):
    vmem = pl.BlockSpec(memory_space=pltpu.VMEM)
    anyspace = pl.BlockSpec(memory_space=pl.ANY)
    dma = pltpu.SemaphoreType.DMA
    bf16 = jnp.bfloat16
    buffers = []
    for row, count in ROWS:
        buffers += ([pltpu.VMEM((4, count, 256), bf16)] * 2 + [pltpu.VMEM((4, count, 512), bf16)] * 2) * 4
    buffers += [pltpu.VMEM((15, count, 512), bf16) for row, count in ROWS]
    return pl.pallas_call(
        reduce_kernel,
        name="reduce_shards",
        out_shape=[
            jax.ShapeDtypeStruct((80, 512), jnp.float32),
            jax.ShapeDtypeStruct((4, 4, 4, 2, 16, 128), bf16),
            jax.ShapeDtypeStruct(edge.shape, edge.dtype),
        ],
        in_specs=[anyspace] * 3,
        out_specs=[vmem, vmem, anyspace],
        scratch_shapes=[pltpu.VMEM((4, 4, 4, 80, 512), bf16)] * 2 + buffers + [
            pltpu.VMEM((16, 128), bf16),
            dma((3, 4)), dma((3, 4)), dma((3, 4)), dma((3, 4, 4)), dma((3, 4, 4)), dma((3, 15)), dma((3, 15)),
            dma((15,)), dma((15,)), dma((8,)), dma((8,)), dma, dma,
        ],
        compiler_params=pltpu.CompilerParams(
            collective_id=2, has_side_effects=True, vmem_limit_bytes=VMEM_LIMIT
        ),
    )(xpart, dpart, edge)


def spread(rows, columns, row_is_plain):
    index = lax.broadcasted_iota(jnp.int32, (rows, columns), 0 if row_is_plain else 1)
    padded = lax.broadcasted_iota(jnp.int32, (rows, columns), 1 if row_is_plain else 0)
    low = 32 * lax.div(lax.rem(index, 128), 16) + 16 * lax.div(index, 128) + lax.rem(index, 16)
    plain = jnp.where(index < 256, low, index)
    device = lax.div(padded, 48)
    inside = padded - 48 * device
    return jnp.where((inside < 36) & (36 * device + inside == plain), 1.0, 0.0).astype(jnp.bfloat16)


def convolve(x_ref, halo_ref, cw_ref, cb_ref, ext):
    tail = halo_ref[...].astype(jnp.float32)
    ext[0:8, :] = jnp.where(lax.axis_index("seq") == 0, 0.0, tail[8:16])
    ext[8:T + 8, :] = x_ref[...].astype(jnp.float32)

    def part(cols):
        pre = cb_ref[:, cols] + cw_ref[0:1, cols] * ext[5:5 + T, cols]
        for k in range(1, 4):
            pre = pre + cw_ref[k:k + 1, cols] * ext[5 + k:5 + k + T, cols]
        gate = logistic(pre)
        act = pre * gate
        return act.astype(jnp.bfloat16), gate + act * (1.0 - gate)

    return part


def conv_kernel(x_ref, halo_ref, cw_ref, cb_ref, w_ref, xc_ref, low_ref, bc_ref, ext, acc):
    i = pl.program_id(0)

    @pl.when(i == 0)
    def _():
        acc[...] = jnp.zeros(acc.shape, jnp.float32)

    part = convolve(x_ref, halo_ref, cw_ref, cb_ref, ext)
    for half in range(2):
        cols = slice(512 * half, 512 * half + 512)
        xc, _ = part(cols)
        xc_ref[:, cols] = xc
        acc[...] += lax.dot_general(
            xc, w_ref[half].reshape(384, 512), (((1,), (1,)), ((), ())), preferred_element_type=jnp.float32
        )

    @pl.when(i == pl.num_programs(0) - 1)
    def _():
        low_ref[...] = jnp.dot(
            acc[...].astype(jnp.bfloat16), spread(384, 256, False), preferred_element_type=jnp.float32
        ).astype(jnp.bfloat16)
        for n in range(32):
            bc_ref[n] = jnp.broadcast_to(acc[:, 340 + n:341 + n], (T, 128))


def conv_project(x, halo, cw, cb, wg):
    E = x.shape[1]
    nat, row, full = tile_specs(1024)
    S = jax.ShapeDtypeStruct
    return pl.pallas_call(
        conv_kernel, grid=(E // 1024,), name="conv_project",
        in_specs=[nat, row(16), row(4), row(1), pl.BlockSpec((2, 8, 48, 512), lambda i: (i, 0, 0, 0))],
        out_specs=[nat, full(T, 256), full(32, T, 128)],
        out_shape=[S((T, E), jnp.bfloat16), S((T, 256), jnp.bfloat16), S((32, T, 128), jnp.float32)],
        scratch_shapes=[pltpu.VMEM((T + 8, 1024), jnp.float32), pltpu.VMEM((T, 384), jnp.float32)],
        compiler_params=pltpu.CompilerParams(vmem_limit_bytes=VMEM_LIMIT),
    )(x, halo, cw, cb, wg)


def grads_kernel(glow_ref, gbc_ref, gcx_ref, x_ref, halo_ref, cw_ref, cb_ref, w_ref, par_ref, ga_ref,
                 gx_ref, head_ref, tail_ref, part_ref, gproj, turned, ext, wide, gext):
    i = pl.program_id(0)
    f32 = jnp.float32

    @pl.when(i == 0)
    def _():
        plain = jnp.concatenate([glow_ref[...], gbc_ref[...]], axis=1).astype(jnp.bfloat16)
        gproj[...] = jnp.dot(plain, spread(288, 384, True), preferred_element_type=f32).astype(jnp.bfloat16)
        turned[...] = gproj[...].T
        gext[T:T + 8, :] = jnp.zeros((8, gext.shape[1]), f32)

    part = convolve(x_ref, halo_ref, cw_ref, cb_ref, ext)
    for half in range(2):
        cols = slice(512 * half, 512 * half + 512)
        xc, slope = part(cols)
        weights = w_ref[half].reshape(384, 512)
        g_conv = (gcx_ref[:, cols] + jnp.dot(gproj[...], weights, preferred_element_type=f32)) * slope
        gext[0:T, cols] = g_conv
        wide[...] = jnp.dot(turned[...], xc, preferred_element_type=f32)

        def put(r, value):
            wide[48 * (r // 3) + 36 + r % 3:48 * (r // 3) + 37 + r % 3, :] = value

        for k in range(4):
            put(k, jnp.sum(g_conv * ext[5 + k:5 + k + T, cols], axis=0, keepdims=True))
        put(4, jnp.sum(g_conv, axis=0, keepdims=True))
        put(5, par_ref[0:1, cols])
        put(6, par_ref[1:2, cols])
        for n in range(N):
            put(7 + n, jnp.concatenate([ga_ref[n, 4 * half + s:4 * half + s + 1, :] for s in range(4)], axis=1))
        part_ref[half] = wide[...].reshape(8, 48, 512).astype(jnp.bfloat16)
    total = cw_ref[0:1, :] * gext[3:3 + T, :]
    for k in range(1, 4):
        total = total + cw_ref[k:k + 1, :] * gext[3 - k:3 - k + T, :]
    gx_ref[...] = total.astype(jnp.bfloat16)
    head_ref[...] = gext[0:8, :]
    tail_ref[...] = gext[T - 16:T, :]


def weight_grads(glow, gbc, gcx, x, halo, cw, cb, wg, par, ga):
    E = x.shape[1]
    nat, row, full = tile_specs(1024)
    S = jax.ShapeDtypeStruct
    f32 = jnp.float32
    block = pl.BlockSpec((2, 8, 48, 512), lambda i: (i, 0, 0, 0))
    return pl.pallas_call(
        grads_kernel, grid=(E // 1024,), name="weight_grads",
        in_specs=[full(T, 256), full(T, 32), nat, nat, row(16), row(4), row(1), block, row(8),
                  pl.BlockSpec((N, 8, 128), lambda i: (0, i, 0))],
        out_specs=[nat, row(8), row(16), block],
        out_shape=[S((T, E), jnp.bfloat16), S((8, E), f32), S((16, E), f32), S((E // 512, 8, 48, 512), jnp.bfloat16)],
        scratch_shapes=[pltpu.VMEM((T, 384), jnp.bfloat16), pltpu.VMEM((384, T), jnp.bfloat16), pltpu.VMEM((T + 8, 1024), f32),
                        pltpu.VMEM((384, 512), f32),
                        pltpu.VMEM((T + 8, 1024), f32)],
        compiler_params=pltpu.CompilerParams(vmem_limit_bytes=VMEM_LIMIT),
    )(glow, gbc, gcx, x, halo, cw, cb, wg, par, ga)


def last_rows_kernel(gx_ref, tail_ref, edge_ref, cw_ref, out_ref, ext):
    ext[0:16, :] = tail_ref[...]
    ext[16:24, :] = jnp.where(lax.axis_index("seq") == 15, 0.0, edge_ref[...])
    total = cw_ref[0:1, :] * ext[3:19, :]
    for k in range(1, 4):
        total = total + cw_ref[k:k + 1, :] * ext[3 - k:19 - k, :]
    out_ref[...] = total.astype(jnp.bfloat16)


def last_rows(gx, tail, edge, cw):
    E = gx.shape[1]
    row = lambda count: pl.BlockSpec((count, 2048), lambda i: (0, i))
    block = pl.BlockSpec((16, 2048), lambda i: (T // 16 - 1, i))
    return pl.pallas_call(
        last_rows_kernel, grid=(E // 2048,), name="last_rows",
        in_specs=[block, row(16), row(8), row(4)], out_specs=block,
        out_shape=jax.ShapeDtypeStruct((T, E), jnp.bfloat16),
        scratch_shapes=[pltpu.VMEM((24, 2048), jnp.float32)],
        input_output_aliases={0: 0},
        compiler_params=pltpu.CompilerParams(vmem_limit_bytes=VMEM_LIMIT),
    )(gx, tail, edge, cw)


def local(x_branch, z_branch, out_grad, x_weight, dt_weight, conv_weight, conv_bias, dt_bias, a_log, d_skip):
    x, z, g = x_branch[0], z_branch[0], out_grad[0]
    E = x.shape[1]
    shard = jnp.concatenate([x_weight.T, jnp.zeros((12, 512), jnp.bfloat16), dt_weight], axis=0)
    gathered, halo = gather(shard, x, tuple(zip(ORDERS, GATHER_ROWS)), 0)
    wg = gathered.reshape(16, 8, 80, 512)
    a2_wide = -jnp.exp(a_log) * LOG2E
    a2 = a2_wide.reshape(N, E // 128, 128)
    a2_blocks = a2_wide.reshape(N, 16, 4, 128).transpose(1, 0, 2, 3).reshape(16, 64, 128)
    bias = conv_bias[None]
    xc, low, bc = conv_project(x, halo, conv_weight, bias, wg)
    step3, drive3, gs3, sig, ends, tot = local_scan(low, wg, xc, z, g, dt_bias[None], a2, bc)
    carried = carry(ends, tot, a2_blocks)
    mixer_out, grad_z, gcx, gdt, par, ga, glow, gbc = main_scan(
        step3, drive3, gs3, sig, xc, z, g, d_skip[None], a2, bc, carried, wg, low
    )
    gx, head, tail, part = weight_grads(glow, jnp.sum(gbc, axis=2), gcx, x, halo, conv_weight, bias, wg, par, ga)
    reduced, params, edge = reduce_all(part.reshape(4, 4, 4, 2, 48, 512), gdt.reshape(4, 4, 4, 2, 32, 512), head)
    grad_x = last_rows(gx, tail, edge, conv_weight)
    params = params.reshape(16, 8, 16, 128)[:, :, :12].reshape(16, 8, 3, 4, 128)
    params = params.transpose(1, 2, 0, 3, 4).reshape(24, E).astype(jnp.float32)
    return (
        mixer_out[None], grad_x[None], grad_z[None], reduced[:36].T, reduced[48:80],
        params[0:4], params[4], params[5], params[7:23], params[6],
    )


def solution(mesh):
    tokens, weights, whole = P("dp", "seq", None), P("seq", "dp"), P()
    in_specs = (tokens,) * 3 + (weights, P("dp", "seq")) + (whole,) * 5
    out_specs = (tokens,) * 3 + (weights, P("dp", "seq")) + (whole,) * 5
    return jax.shard_map(local, mesh=mesh, in_specs=in_specs, out_specs=out_specs, check_vma=False)
```

time: 377 us -> 281 us (0.75)
  Pallas kernels: 350 us -> 266 us
  local copies, waits for them, and re-layouts: 21.2 us -> 7.44 us
    pallas_call x1, Pallas kernels: 107 us -> 78.5 us  [main_scan(): pl.pallas_call(main_scan_kernel, grid=(C,), name='main_scan', in_specs=[t...]
    pallas_call x1, Pallas kernels: 58.5 us -> 32 us  [local_scan(): pl.pallas_call(local_scan_kernel, grid=(C,), name='local_scan', in_specs=...]
    pallas_call x1, Pallas kernels: 77 us -> 54.7 us  [reduce_all(): pl.pallas_call(reduce_kernel, name='reduce_shards', out_shape=[jax.ShapeD...]
    unnamed x34 -> x4, local copies, waits for them, and re-layouts: 13.9 us -> 2.04 us
    pallas_call x1, Pallas kernels: 51.2 us -> 47.2 us  [gather(): pl.pallas_call(functools.partial(gather_kernel, parts, tail is not None),...]
where the time goes in v2:
time: 281 us; the launch traced here: 280 us
  Pallas kernels  266 us (95%)
  local copies, waits for them, and re-layouts  7.44 us (3%)
  other arithmetic  5.56 us (2%)
    pallas_call x1, Pallas kernels, main_scan(): pl.pallas_call(main_scan_kernel, grid=(C,), name='main_scan', in_specs=[t...  78.5 us
    pallas_call x1, Pallas kernels, reduce_all(): pl.pallas_call(reduce_kernel, name='reduce_shards', out_shape=[jax.ShapeD...  54.7 us
    pallas_call x1, Pallas kernels, gather(): pl.pallas_call(functools.partial(gather_kernel, parts, tail is not None),...  47.2 us
    pallas_call x1, Pallas kernels, local_scan(): pl.pallas_call(local_scan_kernel, grid=(C,), name='local_scan', in_specs=...  32 us
    pallas_call x1, Pallas kernels, carry(): pl.pallas_call(carry_kernel, name='carry_exchange', out_shape=jax.ShapeDt...  22.2 us
    pallas_call x1, Pallas kernels, weight_grads(): pl.pallas_call(grads_kernel, grid=(E // 1024,), name='weight_grads', in_s...  16.4 us
    pallas_call x1, Pallas kernels, conv_project(): pl.pallas_call(conv_kernel, grid=(E // 1024,), name='conv_project', in_sp...  11.5 us

profile of v2, /device:TPU:1, one launch (start us, length us, event | category | flops | bytes accessed | tf_op | source)
XLA Modules:
  0.0 279.8 jit_solution(5792297953993947751)
XLA Ops:
  0.7 0.1 pad.1.clone
  0.7 1.5 pad_maximum_fusion.refs_0_
  2.2 1.1 negate_multiply_fusion
  3.4 0.4 reshape.49
  3.7 0.9 copy.25
  4.7 0.9 copy.29
  5.6 47.2 %gather_shards.1 = (bf16[4,4,4,2,80,512]{5,4,3,2,1,0:T(8,128)(2,1)}, bf16[16,8192]{1,0:T(8,128)(2,1)}) custom-call(bf16[80,512]{1,0:T(8,128)(2,1)} %pad_maximum_fusion.refs_0_, bf16[128,8192]{1,0:T(8,128)(2,1)} %bitcast.36), custom_call_target="tpu_custom_call" | custom-call | tf_op jit(solution)/shard_map/gather_shards/pallas_call | solution.py:434
  52.8 11.5 %conv_project.1 = (bf16[128,8192]{1,0:T(8,128)(2,1)}, bf16[128,256]{1,0:T(8,128)(2,1)}, f32[32,128,128]{2,1,0:T(8,128)}) custom-call(bf16[128,8192]{1,0:T(8,128)(2,1)} %bitcast.37, bf16[16,8192]{1,0:T(8,128)(2,1)} %get-tuple-element.36.halo_ref, f32[4,8192]{1,0:T(4,128)} %cw_ref.5, f32[1,8192]{1,0:T(1,128)} %bitcast.51, bf16[16,8,80,512]{3,2,1,0:T(8,128)(2,1)} %bitcast.30), custom_call_target="tpu_custom_call" | custom-call | tf_op jit(solution)/shard_map/conv_project/pallas_call | solution.py:769
  64.3 32.0 %local_scan.1 = (f32[128,64,128]{2,1,0:T(8,128)}, f32[128,64,128]{2,1,0:T(8,128)}, f32[128,64,128]{2,1,0:T(8,128)}, f32[128,8192]{1,0:T(8,128)}, bf16[16,128,128]{2,1,0:T(8,128)(2,1)}, /*index=5*/f32[16,8,128]{2,1,0:T(8,128)}) custom-call(bf16[128,256]{1,0:T(8,128)(2,1)} %get-tuple-element.38.low_ref, bf16[16,8,80,512]{3,2,1,0:T(8,128)(2,1)} %bitcast.31, ...), custom_call_target="tpu_custom_call" | custom-call | tf_op jit(solution)/shard_map/local_scan/pallas_call | solution.py:90
  96.2 22.2 %carry_exchange.1.ent_ref = bf16[16,128,128]{2,1,0:T(8,128)(2,1)} custom-call(bf16[16,128,128]{2,1,0:T(8,128)(2,1)} %get-tuple-element.45.ends, f32[16,8,128]{2,1,0:T(8,128)} %get-tuple-element.46.tot, f32[16,64,128]{2,1,0:T(8,128)} %bitcast.47), custom_call_target="tpu_custom_call" | custom-call | tf_op jit(solution)/shard_map/carry_exchange/pallas_call | solution.py:492
  118.4 78.5 %main_scan.1 = (bf16[128,8192]{1,0:T(8,128)(2,1)}, bf16[128,8192]{1,0:T(8,128)(2,1)}, f32[128,8192]{1,0:T(8,128)}, bf16[16,8,32,512]{3,2,1,0:T(8,128)(2,1)}, f32...) custom-call(f32[128,64,128]{2,1,0:T(8,128)} %get-tuple-element.41.step_ref, ...), custom_call_target="tpu_custom_call" | custom-call | tf_op jit(solution)/shard_map/main_scan/pallas_call | solution.py:242
  196.9 2.8 %reduce_sum.9.gbc_ref = f32[128,32]{1,0:T(8,128)} reduce(f32[128,32,128]{2,1,0:T(8,128)} %get-tuple-element.49, f32[]{:T(128)} %constant.2.clone.1), dimensions={2}, to_apply=%region_0.0 | reduce | flops 520192 | bytes 2113540 | tf_op jit(solution)/shard_map/reduce_sum | solution.py:877
  199.8 16.4 %weight_grads.1 = (bf16[128,8192]{1,0:T(8,128)(2,1)}, f32[8,8192]{1,0:T(8,128)}, f32[16,8192]{1,0:T(8,128)}, bf16[16,8,48,512]{3,2,1,0:T(8,128)(2,1)}) custom-call(f32[128,256]{1,0:T(8,128)} %get-tuple-element.48.glow_ref, f32[128,32]{1,0:T(8,128)} %reduce_sum.9.gbc_ref, f32[128,8192]{1,0:T(8,128)} %get-tuple-element.50.gcx_ref, bf16[128,8192]{1,0:T(8,128)(2,1)} %bitcast.38, ...), custom_call_target="tpu_custom_call" | custom-call | tf_op jit(solution)/shard_map/weight_grads/pallas_call | solution.py:825
  216.2 54.7 %reduce_shards.1 = (f32[80,512]{1,0:T(8,128)}, bf16[4,4,4,2,16,128]{5,4,3,2,1,0:T(8,128)(2,1)}, f32[8,8192]{1,0:T(8,128)}) custom-call(bf16[4,4,4,2,48,512]{5,4,3,2,1,0:T(8,128)(2,1)} %bitcast.43, bf16[4,4,4,2,32,512]{5,4,3,2,1,0:T(8,128)(2,1)} %bitcast.46, f32[8,8192]{1,0:T(8,128)} %get-tuple-element.57.edge), custom_call_target="tpu_custom_call" | custom-call | tf_op jit(solution)/shard_map/reduce_shards/pallas_call | solution.py:693
  270.9 1.1 copy.28
  272.1 0.0 copy-start
  272.1 3.5 %last_rows.1 = bf16[128,8192]{1,0:T(8,128)(2,1)} custom-call(bf16[128,8192]{1,0:T(8,128)(2,1)} %get-tuple-element.53.gx_ref, f32[16,8192]{1,0:T(8,128)} %get-tuple-element.54.tail_ref, f32[8,8192]{1,0:T(8,128)} %get-tuple-element.58.edge_ref, f32[4,8192]{1,0:T(4,128)} %cw_ref.5), custom_call_target="tpu_custom_call", output_to_operand_aliasing={{}: (0, {})} | custom-call | tf_op jit(solution)/shard_map/last_rows/pallas_call | solution.py:851
  275.6 0.0 copy-done
  275.6 0.6 slice.25
  276.3 0.6 slice_bitcast_fusion
  276.9 0.1 convert_bitcast_fusion
  277.0 0.2 copy.27
  277.2 0.3 reshape.54
  277.6 0.7 fusion.1
  278.3 0.7 slice.33
  278.9 0.8 slice.36
  (1 shorter events, 0.0 us)
Async XLA Ops:
  272.1 3.5 %copy-start = (f32[80,512]{1,0:T(8,128)S(1)}, f32[80,512]{1,0:T(8,128)}, u32[]{:S(2)}) copy-start(f32[80,512]{1,0:T(8,128)} %get-tuple-element.60) | copy-start | bytes 491524

commit v3 on v2

--- a/solution.py
+++ b/solution.py
@@ -13,6 +13,7 @@
 LOG2E = 1.4426950408889634
 VMEM_LIMIT = 62 * 2**20
 LOCAL_GROUP, LOCAL_UNROLL = 4, 16
+SHIPMENTS = ((0, 4), (4, 3), (7, 1))
 CHUNKS = 1
 FWD_GROUP, FWD_UNROLL = 8, 8
 BWD_GROUP, BWD_UNROLL = 8, 8
@@ -29,8 +30,19 @@
     return nat, row, full
 
 
-def local_scan_kernel(low_ref, wa_ref, wb_ref, x_ref, z_ref, g_ref, bias_ref, a2_ref, bc_ref,
-                      step_ref, drive_ref, gs_ref, sig_ref, ends_ref, tot_ref, scr):
+def local_scan_kernel(low_ref, wa_ref, wb_ref, x_ref, z_ref, g_ref, bias_ref, a2_ref, bc_ref, rates_ref,
+                      step_ref, drive_ref, gs_ref, sig_ref, carried, ends_all, got, back,
+                      ssem, rsem, bsend, brecv, own_sem):
+    i = pl.program_id(0)
+    d, j, _, _ = place()
+    others = [lax.rem(j + k, 16) for k in range(1, 16)]
+
+    @pl.when(i == 0)
+    def _():
+        barrier = pltpu.get_barrier_semaphore()
+        for k in others:
+            pl.semaphore_signal(barrier, inc=1, device_id=(d, k), device_id_type=MESH)
+
     low = low_ref[...]
     rows = [ref.reshape(T * 8, 128) for ref in (step_ref, drive_ref, gs_ref)]
     for half in range(2):
@@ -71,14 +83,72 @@
         tot, e, _, l = lax.fori_loop(0, T // LOCAL_UNROLL, body, (zero, (zero,) * many, (one,) * many, (zero,) * many))
         ends += e
         lams += l
+    high = tot.astype(jnp.bfloat16)
+    sums = jnp.concatenate([high.astype(jnp.float32), tot - high.astype(jnp.float32)], axis=0).astype(jnp.bfloat16)
     for n in range(N):
-        for half in range(2):
-            scr[half, 4 * n:4 * n + 4, :] = ends[n][4 * half:4 * half + 4]
-            scr[half, 64 + 4 * n:64 + 4 * n + 4, :] = lams[n][4 * half:4 * half + 4]
-    ends_ref[...] = scr[...].astype(jnp.bfloat16)
-    for half in range(2):
-        tot_ref[half, 0:4, :] = tot[4 * half:4 * half + 4]
-        tot_ref[half, 4:8, :] = jnp.zeros((4, 128), jnp.float32)
+        ends_all[n, i, 0:16, :] = jnp.concatenate([ends[n], lams[n]], axis=0).astype(jnp.bfloat16)
+        ends_all[n, i, 16:32, :] = sums
+
+    def chunks(group):
+        return pl.ds(SHIPMENTS[group][0], SHIPMENTS[group][1])
+
+    def outgoing(group, to):
+        return remote(ends_all.at[to, chunks(group)], got.at[j, chunks(group)], ssem.at[group, to], rsem.at[group, j], (d, to))
+
+    def returned(group, to):
+        return remote(back.at[to, chunks(group)], carried.at[j, chunks(group)], bsend.at[group, to], brecv.at[group, j], (d, to))
+
+    def ship(group):
+        for to in others:
+            outgoing(group, to).start()
+        first, count = SHIPMENTS[group]
+        for k in range(first, first + count):
+            got[j, k] = ends_all[j, k]
+
+    def recur(group):
+        for source in others:
+            there = got.at[source, chunks(group)]
+            remote(there, there, ssem.at[group, source], rsem.at[group, source], (d, source)).wait_recv()
+        first, count = SHIPMENTS[group]
+        for c in range(first, first + count):
+            rates = rates_ref[j, 8 * c:8 * c + 8, :]
+            blocks = [got[k, c].astype(jnp.float32) for k in range(16)]
+            decays = [jnp.exp2(rates * (block[16:24] + block[24:32])) for block in blocks]
+            enter, leave = [jnp.zeros((8, 128), jnp.float32)], [jnp.zeros((8, 128), jnp.float32)]
+            for k in range(15):
+                enter.append(decays[k] * enter[k] + blocks[k][0:8])
+                leave.append(decays[15 - k] * leave[k] + blocks[15 - k][8:16])
+            for k in range(16):
+                back[k, c] = jnp.concatenate([enter[k], leave[15 - k]], axis=0).astype(jnp.bfloat16)
+        for to in others:
+            returned(group, to).start()
+        pltpu.make_async_copy(back.at[j, chunks(group)], carried.at[j, chunks(group)], own_sem.at[group]).start()
+
+    @pl.when(i == 3)
+    def _():
+        pl.semaphore_wait(pltpu.get_barrier_semaphore(), 15)
+        ship(0)
+
+    @pl.when(i == 5)
+    def _():
+        recur(0)
+
+    @pl.when(i == 6)
+    def _():
+        ship(1)
+
+    @pl.when(i == 7)
+    def _():
+        ship(2)
+        recur(1)
+        recur(2)
+        for group in range(3):
+            pltpu.make_async_copy(back.at[j, chunks(group)], carried.at[j, chunks(group)], own_sem.at[group]).wait()
+            for k in others:
+                there = carried.at[k, chunks(group)]
+                remote(there, there, bsend.at[group, k], brecv.at[group, k], (d, k)).wait_recv()
+                outgoing(group, k).wait_send()
+                returned(group, k).wait_send()
 
 
 def local_scan(low, wg, x_conv, z, g, bias, a2, bc):
@@ -91,20 +161,19 @@
         local_scan_kernel, grid=(C,), name="local_scan",
         in_specs=[full(T, 256), pl.BlockSpec((2, 8, 16, 512), lambda i: (i, 0, 3, 0)),
                   pl.BlockSpec((2, 8, 16, 512), lambda i: (i, 0, 4, 0)), nat, nat, nat,
-                  row(1), pl.BlockSpec((N, 8, 128), lambda i: (0, i, 0)), full(32, T, 128)],
-        out_specs=[tri, tri, tri, nat, pl.BlockSpec((2, 128, 128), lambda i: (i, 0, 0)),
-                   pl.BlockSpec((2, 8, 128), lambda i: (i, 0, 0))],
+                  row(1), pl.BlockSpec((N, 8, 128), lambda i: (0, i, 0)), full(32, T, 128), full(N, E // 128, 128)],
+        out_specs=[tri, tri, tri, nat, pl.BlockSpec(memory_space=pl.ANY)],
         out_shape=[jax.ShapeDtypeStruct((T, E // 128, 128), f32)] * 3 + [
-            jax.ShapeDtypeStruct((T, E), f32), jax.ShapeDtypeStruct((2 * C, 128, 128), jnp.bfloat16),
-            jax.ShapeDtypeStruct((2 * C, 8, 128), f32)],
-        scratch_shapes=[pltpu.VMEM((2, 128, 128), f32)],
-        compiler_params=pltpu.CompilerParams(vmem_limit_bytes=VMEM_LIMIT),
-    )(low, wg, wg, x_conv, z, g, bias, a2, bc)
+            jax.ShapeDtypeStruct((T, E), f32), jax.ShapeDtypeStruct((16, C, 16, 128), jnp.bfloat16)],
+        scratch_shapes=[pltpu.VMEM((16, C, 32, 128), jnp.bfloat16)] * 2 + [pltpu.VMEM((16, C, 16, 128), jnp.bfloat16)]
+        + [pltpu.SemaphoreType.DMA((3, 16))] * 4 + [pltpu.SemaphoreType.DMA((3,))],
+        compiler_params=pltpu.CompilerParams(collective_id=1, has_side_effects=True, vmem_limit_bytes=VMEM_LIMIT),
+    )(low, wg, wg, x_conv, z, g, bias, a2, bc, a2)
 
 
 def main_scan_kernel(step_ref, drive_ref, gs_ref, sig_ref, x_ref, z_ref, g_ref, dskip_ref, a2_ref, bc_ref, ent_ref, wa_ref, wb_ref, low_ref,
               mix_ref, gz_ref, gcx_ref, gdt_ref, par_ref, ga_ref, glow_ref, gbc_ref,
-              es, us, y3, gd3, gr3, accb, accc, alow, turned):
+              es, us, y3, gd3, gr3, accb, accc, alow, turned, both):
     i = pl.program_id(0)
     f32 = jnp.float32
     span = [slice(8 * q, 8 * q + 8) for q in range(CHUNKS)]
@@ -119,8 +188,7 @@
     es[...] = ent_ref[...].astype(f32)
 
     def state(base, n, q):
-        rows = slice(base + 4 * n, base + 4 * n + 4)
-        return jnp.concatenate([es[2 * q, rows, :], es[2 * q + 1, rows, :]], axis=0)
+        return es[n, q, base:base + 8, :]
 
     def add(total, term):
         return term if total is None else total + term
@@ -186,7 +254,7 @@
                 adj, ra = tuple(na), tuple(nr)
             return adj, ra
 
-        _, ra = lax.fori_loop(0, T // BWD_UNROLL, backward, (tuple(state(64, n, q) for n in group for q in range(CHUNKS)), (zero,) * (BWD_GROUP * CHUNKS)))
+        _, ra = lax.fori_loop(0, T // BWD_UNROLL, backward, (tuple(state(8, n, q) for n in group for q in range(CHUNKS)), (zero,) * (BWD_GROUP * CHUNKS)))
         for p, n in enumerate(group):
             for q in range(CHUNKS):
                 ga_ref[n, span[q]] = ra[p * CHUNKS + q] * a2_ref[n, span[q]] * LN2
@@ -223,10 +291,12 @@
         glow_ref[...] = alow[...]
 
         def fold(t, _):
-            gbc_ref[t, 0:16, :] = jnp.sum(accb[t], axis=1)
-            gbc_ref[t, 16:32, :] = jnp.sum(accc[t], axis=1)
+            both[t, 0:16, :] = jnp.sum(accb[t], axis=1)
+            both[t, 16:32, :] = jnp.sum(accc[t], axis=1)
             return 0
         lax.fori_loop(0, T, fold, 0)
+        for n in range(2 * N):
+            gbc_ref[:, n:n + 1] = jnp.sum(both.reshape(T * 32, 128)[pl.ds(n, T, stride=32), :], axis=1, keepdims=True)
 
 def main_scan(step3, drive3, gs3, sig, x_conv, z, g, dskip, a2, bc, ent, wg, low):
     E = x_conv.shape[1]
@@ -242,15 +312,16 @@
     return pl.pallas_call(
         main_scan_kernel, grid=(C,), name="main_scan",
         in_specs=[tri, tri, tri, nat, nat, nat, nat, row(1), rate, once(32, T, 128),
-                  pl.BlockSpec((2 * CHUNKS, 128, 128), lambda i: (i, 0, 0)),
+                  pl.BlockSpec((N, CHUNKS, 16, 128), lambda i: (0, i, 0, 0)),
                   pl.BlockSpec((2 * CHUNKS, 8, 16, 512), lambda i: (i, 0, 3, 0)),
                   pl.BlockSpec((2 * CHUNKS, 8, 16, 512), lambda i: (i, 0, 4, 0)), once(T, 256)],
         out_specs=[nat, nat, nat, pl.BlockSpec((2 * CHUNKS, 8, 32, 512), lambda i: (i, 0, 0, 0)),
-                   row(8), rate, full(T, 256), full(T, 32, 128)],
+                   row(8), rate, full(T, 256), full(T, 32)],
         out_shape=[S((T, E), jnp.bfloat16), S((T, E), jnp.bfloat16), S((T, E), f32), S((E // 512, 8, 32, 512), jnp.bfloat16),
-                   S((8, E), f32), S((N, E // 128, 128), f32), S((T, 256), f32), S((T, 32, 128), f32)],
-        scratch_shapes=[pltpu.VMEM((2 * CHUNKS, 128, 128), f32), pltpu.VMEM((T, N, 8 * CHUNKS, 128), f32)]
-        + [pltpu.VMEM((T, 8 * CHUNKS, 128), f32)] * 3 + [pltpu.VMEM((T, N, 8, 128), f32)] * 2 + [pltpu.VMEM((T, 256), f32), pltpu.VMEM((256, T), jnp.bfloat16)],
+                   S((8, E), f32), S((N, E // 128, 128), f32), S((T, 256), f32), S((T, 32), f32)],
+        scratch_shapes=[pltpu.VMEM((N, CHUNKS, 16, 128), f32), pltpu.VMEM((T, N, 8 * CHUNKS, 128), f32)]
+        + [pltpu.VMEM((T, 8 * CHUNKS, 128), f32)] * 3 + [pltpu.VMEM((T, N, 8, 128), f32)] * 2 + [pltpu.VMEM((T, 256), f32), pltpu.VMEM((256, T), jnp.bfloat16),
+           pltpu.VMEM((T, 32, 128), f32)],
         compiler_params=pltpu.CompilerParams(vmem_limit_bytes=VMEM_LIMIT),
     )(step3, drive3, gs3, sig, x_conv, z, g, dskip, a2, bc, ent, wg, wg, low)
 
@@ -385,7 +456,7 @@
             for p in count:
                 go(direct(p, k))
     if with_tail:
-        tail_copy = remote(tail_ref.at[pl.ds(T - 16, 16), :], halo, hsend, hrecv, following)
+        tail_copy = remote(tail_ref, halo, hsend, hrecv, following)
         go(tail_copy)
     local.wait()
     for i in range(4):
@@ -428,7 +499,7 @@
     sems = [dma, dma((count, 4, 4)), dma((count, 4, 4)), dma((count, 15)), dma((count, 15)), dma((count, 4, 4)), dma((count, 4, 4))]
     operands = [shard]
     if tail is not None:
-        out_shape.append(jax.ShapeDtypeStruct((16, tail.shape[1]), tail.dtype))
+        out_shape.append(jax.ShapeDtypeStruct(tail.shape, tail.dtype))
         sems += [dma, dma]
         operands.append(tail)
     return pl.pallas_call(
@@ -440,71 +511,6 @@
         scratch_shapes=sems,
         compiler_params=pltpu.CompilerParams(collective_id=collective_id, has_side_effects=True, vmem_limit_bytes=VMEM_LIMIT),
     )(*operands)
-
-
-def carry_kernel(ends, tot, a2, out, got, got_tot, back, ssem, rsem, tsend, trecv, bsend, brecv):
-    d, j, pos, core = place()
-    peers = [(d, lax.rem(j + k, 16)) for k in range(1, 16)]
-    greet(peers)
-    sent = []
-    for k in range(1, 16):
-        to = lax.rem(j + k, 16)
-        one = remote(ends.at[to], got.at[j], ssem.at[k], rsem.at[k], peers[k - 1])
-        two = remote(tot.at[to], got_tot.at[j], tsend.at[k], trecv.at[k], peers[k - 1])
-        one.start()
-        two.start()
-        sent += [one, two]
-    got[j] = ends[j]
-    got_tot[j] = tot[j]
-    for k in range(1, 16):
-        source = lax.rem(j + 16 - k, 16)
-        remote(got.at[source], got.at[source], ssem.at[k], rsem.at[k], peers[k - 1]).wait_recv()
-        remote(got_tot.at[source], got_tot.at[source], tsend.at[k], trecv.at[k], peers[k - 1]).wait_recv()
-    rates = a2[j]
-
-    def decay(i):
-        return jnp.exp2(rates * jnp.concatenate([got_tot[i, 0:4, :]] * 16, axis=0))
-
-    enter = jnp.zeros((64, 128), jnp.float32)
-    leave = jnp.zeros((64, 128), jnp.float32)
-    for i in range(16):
-        back[i, 0:64, :] = enter.astype(jnp.bfloat16)
-        enter = decay(i) * enter + got[i, 0:64, :].astype(jnp.float32)
-        r = 15 - i
-        back[r, 64:128, :] = leave.astype(jnp.bfloat16)
-        leave = decay(r) * leave + got[r, 64:128, :].astype(jnp.float32)
-    for k in range(1, 16):
-        to = lax.rem(j + k, 16)
-        one = remote(back.at[to], out.at[j], bsend.at[k], brecv.at[k], peers[k - 1])
-        one.start()
-        sent.append(one)
-    out[j] = back[j]
-    for k in range(1, 16):
-        source = lax.rem(j + 16 - k, 16)
-        remote(out.at[source], out.at[source], bsend.at[k], brecv.at[k], peers[k - 1]).wait_recv()
-    for copy in sent:
-        copy.wait_send()
-
-
-def carry(ends, tot, a2):
-    vmem = pl.BlockSpec(memory_space=pltpu.VMEM)
-    dma = pltpu.SemaphoreType.DMA((16,))
-    return pl.pallas_call(
-        carry_kernel,
-        name="carry_exchange",
-        out_shape=jax.ShapeDtypeStruct((16, 128, 128), jnp.bfloat16),
-        in_specs=[vmem] * 3,
-        out_specs=vmem,
-        scratch_shapes=[
-            pltpu.VMEM((16, 128, 128), jnp.bfloat16),
-            pltpu.VMEM((16, 8, 128), jnp.float32),
-            pltpu.VMEM((16, 128, 128), jnp.bfloat16),
-            dma, dma, dma, dma, dma, dma,
-        ],
-        compiler_params=pltpu.CompilerParams(
-            collective_id=1, has_side_effects=True, vmem_limit_bytes=VMEM_LIMIT
-        ),
-    )(ends, tot, a2)
 
 
 def reduce_kernel(xpart, dpart, edge, out, all_params, halo, sums, cross, *scratch):
@@ -721,9 +727,14 @@
     return jnp.where((inside < 36) & (36 * device + inside == plain), 1.0, 0.0).astype(jnp.bfloat16)
 
 
+HALO = pl.BlockSpec((3, 8, 128), lambda i: (0, i, 0))
+
+
 def convolve(x_ref, halo_ref, cw_ref, cb_ref, ext):
-    tail = halo_ref[...].astype(jnp.float32)
-    ext[0:8, :] = jnp.where(lax.axis_index("seq") == 0, 0.0, tail[8:16])
+    first = lax.axis_index("seq") == 0
+    for r in range(3):
+        for s in range(8):
+            ext[5 + r:6 + r, 128 * s:128 * s + 128] = jnp.where(first, 0.0, halo_ref[r, s:s + 1, :])
     ext[8:T + 8, :] = x_ref[...].astype(jnp.float32)
 
     def part(cols):
@@ -768,7 +779,7 @@
     S = jax.ShapeDtypeStruct
     return pl.pallas_call(
         conv_kernel, grid=(E // 1024,), name="conv_project",
-        in_specs=[nat, row(16), row(4), row(1), pl.BlockSpec((2, 8, 48, 512), lambda i: (i, 0, 0, 0))],
+        in_specs=[nat, HALO, row(4), row(1), pl.BlockSpec((2, 8, 48, 512), lambda i: (i, 0, 0, 0))],
         out_specs=[nat, full(T, 256), full(32, T, 128)],
         out_shape=[S((T, E), jnp.bfloat16), S((T, 256), jnp.bfloat16), S((32, T, 128), jnp.float32)],
         scratch_shapes=[pltpu.VMEM((T + 8, 1024), jnp.float32), pltpu.VMEM((T, 384), jnp.float32)],
@@ -812,7 +823,9 @@
     for k in range(1, 4):
         total = total + cw_ref[k:k + 1, :] * gext[3 - k:3 - k + T, :]
     gx_ref[...] = total.astype(jnp.bfloat16)
-    head_ref[...] = gext[0:8, :]
+    for r in range(3):
+        for s in range(8):
+            head_ref[r, s:s + 1, :] = gext[r:r + 1, 128 * s:128 * s + 128]
     tail_ref[...] = gext[T - 16:T, :]
 
 
@@ -824,10 +837,10 @@
     block = pl.BlockSpec((2, 8, 48, 512), lambda i: (i, 0, 0, 0))
     return pl.pallas_call(
         grads_kernel, grid=(E // 1024,), name="weight_grads",
-        in_specs=[full(T, 256), full(T, 32), nat, nat, row(16), row(4), row(1), block, row(8),
+        in_specs=[full(T, 256), full(T, 32), nat, nat, HALO, row(4), row(1), block, row(8),
                   pl.BlockSpec((N, 8, 128), lambda i: (0, i, 0))],
-        out_specs=[nat, row(8), row(16), block],
-        out_shape=[S((T, E), jnp.bfloat16), S((8, E), f32), S((16, E), f32), S((E // 512, 8, 48, 512), jnp.bfloat16)],
+        out_specs=[nat, HALO, row(16), block],
+        out_shape=[S((T, E), jnp.bfloat16), S((3, E // 128, 128), f32), S((16, E), f32), S((E // 512, 8, 48, 512), jnp.bfloat16)],
         scratch_shapes=[pltpu.VMEM((T, 384), jnp.bfloat16), pltpu.VMEM((384, T), jnp.bfloat16), pltpu.VMEM((T + 8, 1024), f32),
                         pltpu.VMEM((384, 512), f32),
                         pltpu.VMEM((T + 8, 1024), f32)],
@@ -837,7 +850,10 @@
 
 def last_rows_kernel(gx_ref, tail_ref, edge_ref, cw_ref, out_ref, ext):
     ext[0:16, :] = tail_ref[...]
-    ext[16:24, :] = jnp.where(lax.axis_index("seq") == 15, 0.0, edge_ref[...])
+    last = lax.axis_index("seq") == 15
+    for r in range(3):
+        for s in range(edge_ref.shape[1]):
+            ext[16 + r:17 + r, 128 * s:128 * s + 128] = jnp.where(last, 0.0, edge_ref[r, s:s + 1, :])
     total = cw_ref[0:1, :] * ext[3:19, :]
     for k in range(1, 4):
         total = total + cw_ref[k:k + 1, :] * ext[3 - k:19 - k, :]
@@ -846,13 +862,13 @@
 
 def last_rows(gx, tail, edge, cw):
     E = gx.shape[1]
-    row = lambda count: pl.BlockSpec((count, 2048), lambda i: (0, i))
-    block = pl.BlockSpec((16, 2048), lambda i: (T // 16 - 1, i))
+    full = lambda *shape: pl.BlockSpec(shape, lambda i: (0,) * len(shape))
+    block = pl.BlockSpec((16, E), lambda i: (T // 16 - 1, 0))
     return pl.pallas_call(
-        last_rows_kernel, grid=(E // 2048,), name="last_rows",
-        in_specs=[block, row(16), row(8), row(4)], out_specs=block,
+        last_rows_kernel, grid=(1,), name="last_rows",
+        in_specs=[block, full(16, E), full(3, E // 128, 128), full(4, E)], out_specs=block,
         out_shape=jax.ShapeDtypeStruct((T, E), jnp.bfloat16),
-        scratch_shapes=[pltpu.VMEM((24, 2048), jnp.float32)],
+        scratch_shapes=[pltpu.VMEM((24, E), jnp.float32)],
         input_output_aliases={0: 0},
         compiler_params=pltpu.CompilerParams(vmem_limit_bytes=VMEM_LIMIT),
     )(gx, tail, edge, cw)
@@ -862,19 +878,17 @@
     x, z, g = x_branch[0], z_branch[0], out_grad[0]
     E = x.shape[1]
     shard = jnp.concatenate([x_weight.T, jnp.zeros((12, 512), jnp.bfloat16), dt_weight], axis=0)
-    gathered, halo = gather(shard, x, tuple(zip(ORDERS, GATHER_ROWS)), 0)
+    gathered, halo = gather(shard, x[T - 3:].astype(jnp.float32).reshape(3, E // 128, 128), tuple(zip(ORDERS, GATHER_ROWS)), 0)
     wg = gathered.reshape(16, 8, 80, 512)
     a2_wide = -jnp.exp(a_log) * LOG2E
     a2 = a2_wide.reshape(N, E // 128, 128)
-    a2_blocks = a2_wide.reshape(N, 16, 4, 128).transpose(1, 0, 2, 3).reshape(16, 64, 128)
     bias = conv_bias[None]
     xc, low, bc = conv_project(x, halo, conv_weight, bias, wg)
-    step3, drive3, gs3, sig, ends, tot = local_scan(low, wg, xc, z, g, dt_bias[None], a2, bc)
-    carried = carry(ends, tot, a2_blocks)
+    step3, drive3, gs3, sig, carried = local_scan(low, wg, xc, z, g, dt_bias[None], a2, bc)
     mixer_out, grad_z, gcx, gdt, par, ga, glow, gbc = main_scan(
         step3, drive3, gs3, sig, xc, z, g, d_skip[None], a2, bc, carried, wg, low
     )
-    gx, head, tail, part = weight_grads(glow, jnp.sum(gbc, axis=2), gcx, x, halo, conv_weight, bias, wg, par, ga)
+    gx, head, tail, part = weight_grads(glow, gbc, gcx, x, halo, conv_weight, bias, wg, par, ga)
     reduced, params, edge = reduce_all(part.reshape(4, 4, 4, 2, 48, 512), gdt.reshape(4, 4, 4, 2, 32, 512), head)
     grad_x = last_rows(gx, tail, edge, conv_weight)
     params = params.reshape(16, 8, 16, 128)[:, :, :12].reshape(16, 8, 3, 4, 128)

time: 281 us -> 266 us (0.947)
  Pallas kernels: 266 us -> 254 us
    pallas_call x2 -> x1, Pallas kernels: 25.7 us -> 2.82 us  [last_rows(): pl.pallas_call(last_rows_kernel, grid=(1,), name='last_rows', in_specs=[b...]
    pallas_call x1, Pallas kernels: 32 us -> 45.7 us  [local_scan(): pl.pallas_call(local_scan_kernel, grid=(C,), name='local_scan', in_specs=...]
    pallas_call x1, Pallas kernels: 47.2 us -> 43.6 us  [gather(): pl.pallas_call(functools.partial(gather_kernel, parts, tail is not None),...]
    reduce_sum x1 -> x0, other arithmetic: 2.84 us -> none  [local(): jnp.sum(gbc, axis=2)]
where the time goes in v3:
time: 266 us; the launch traced here: 265 us
  Pallas kernels  254 us (95%)
  local copies, waits for them, and re-layouts  6.81 us (3%)
  other arithmetic  3.65 us (1%)
    pallas_call x1, Pallas kernels, main_scan(): pl.pallas_call(main_scan_kernel, grid=(C,), name='main_scan', in_specs=[t...  79.4 us
    pallas_call x1, Pallas kernels, reduce_all(): pl.pallas_call(reduce_kernel, name='reduce_shards', out_shape=[jax.ShapeD...  54.3 us
    pallas_call x1, Pallas kernels, local_scan(): pl.pallas_call(local_scan_kernel, grid=(C,), name='local_scan', in_specs=...  45.7 us
    pallas_call x1, Pallas kernels, gather(): pl.pallas_call(functools.partial(gather_kernel, parts, tail is not None),...  43.6 us
    pallas_call x1, Pallas kernels, weight_grads(): pl.pallas_call(grads_kernel, grid=(E // 1024,), name='weight_grads', in_s...  16.4 us
    pallas_call x1, Pallas kernels, conv_project(): pl.pallas_call(conv_kernel, grid=(E // 1024,), name='conv_project', in_sp...  11.5 us

profile of v3, /device:TPU:1, one launch (start us, length us, event | category | flops | bytes accessed | tf_op | source)
XLA Modules:
  0.0 264.9 jit_solution(12831726855771605341)
XLA Ops:
  0.7 0.1 pad.1.clone
  0.7 1.5 pad_maximum_fusion.refs_0_
  2.2 0.9 convert_bitcast_fusion.1
  3.2 0.6 copy.29
  3.8 1.1 multiply_bitcast_fusion
  4.9 0.9 copy.27
  5.8 43.6 %gather_shards.1 = (bf16[4,4,4,2,80,512]{5,4,3,2,1,0:T(8,128)(2,1)}, f32[3,64,128]{2,1,0:T(8,128)}) custom-call(bf16[80,512]{1,0:T(8,128)(2,1)} %pad_maximum_fusion.refs_0_, f32[3,64,128]{2,1,0:T(8,128)} %bitcast.53), custom_call_target="tpu_custom_call" | custom-call | tf_op jit(solution)/shard_map/gather_shards/pallas_call | solution.py:505
  49.5 11.5 %conv_project.1 = (bf16[128,8192]{1,0:T(8,128)(2,1)}, bf16[128,256]{1,0:T(8,128)(2,1)}, f32[32,128,128]{2,1,0:T(8,128)}) custom-call(bf16[128,8192]{1,0:T(8,128)(2,1)} %bitcast.39, f32[3,64,128]{2,1,0:T(8,128)} %get-tuple-element.35.halo_ref, f32[4,8192]{1,0:T(4,128)} %cw_ref.5, f32[1,8192]{1,0:T(1,128)} %bitcast.54, bf16[16,8,80,512]{3,2,1,0:T(8,128)(2,1)} %bitcast.33), custom_call_target="tpu_custom_call" | custom-call | tf_op jit(solution)/shard_map/conv_project/pallas_call | solution.py:780
  60.9 45.7 %local_scan.1 = (f32[128,64,128]{2,1,0:T(8,128)}, f32[128,64,128]{2,1,0:T(8,128)}, f32[128,64,128]{2,1,0:T(8,128)}, f32[128,8192]{1,0:T(8,128)}, bf16[16,8,16,128]{3,2,1,0:T(8,128)(2,1)}) custom-call(bf16[128,256]{1,0:T(8,128)(2,1)} %get-tuple-element.37.low_ref, bf16[16,8,80,512]{3,2,1,0:T(8,128)(2,1)} %bitcast.34, bf16[16,8,80,512]{3,2,1,0:T(8,128)(2,1)} %bitcast.35, ...), custom_call_target="tpu_custom_call" | custom-call | tf_op jit(solution)/shard_map/local_scan/pallas_call | solution.py:160
  106.6 79.4 %main_scan.1 = (bf16[128,8192]{1,0:T(8,128)(2,1)}, bf16[128,8192]{1,0:T(8,128)(2,1)}, f32[128,8192]{1,0:T(8,128)}, bf16[16,8,32,512]{3,2,1,0:T(8,128)(2,1)}, f32...) custom-call(f32[128,64,128]{2,1,0:T(8,128)} %get-tuple-element.40.step_ref, ...), custom_call_target="tpu_custom_call" | custom-call | tf_op jit(solution)/shard_map/main_scan/pallas_call | solution.py:312
  186.1 16.4 %weight_grads.1 = (bf16[128,8192]{1,0:T(8,128)(2,1)}, f32[3,64,128]{2,1,0:T(8,128)}, f32[16,8192]{1,0:T(8,128)}, bf16[16,8,48,512]{3,2,1,0:T(8,128)(2,1)}) custom-call(f32[128,256]{1,0:T(8,128)} %get-tuple-element.46.glow_ref, f32[128,32]{1,0:T(8,128)} %get-tuple-element.47.gbc_ref, f32[128,8192]{1,0:T(8,128)} %get-tuple-element.48.gcx_ref, ...), custom_call_target="tpu_custom_call" | custom-call | tf_op jit(solution)/shard_map/weight_grads/pallas_call | solution.py:838
  202.5 54.3 %reduce_shards.1 = (f32[80,512]{1,0:T(8,128)}, bf16[4,4,4,2,16,128]{5,4,3,2,1,0:T(8,128)(2,1)}, f32[3,64,128]{2,1,0:T(8,128)}) custom-call(bf16[4,4,4,2,48,512]{5,4,3,2,1,0:T(8,128)(2,1)} %bitcast.48, bf16[4,4,4,2,32,512]{5,4,3,2,1,0:T(8,128)(2,1)} %bitcast.49, f32[3,64,128]{2,1,0:T(8,128)} %get-tuple-element.55.edge), custom_call_target="tpu_custom_call" | custom-call | tf_op jit(solution)/shard_map/reduce_shards/pallas_call | solution.py:699
  256.8 1.1 copy.25
  257.9 0.0 copy-start
  257.9 2.8 %last_rows.1 = bf16[128,8192]{1,0:T(8,128)(2,1)} custom-call(bf16[128,8192]{1,0:T(8,128)(2,1)} %get-tuple-element.51.gx_ref, f32[16,8192]{1,0:T(8,128)} %get-tuple-element.52.tail_ref, f32[3,64,128]{2,1,0:T(8,128)} %get-tuple-element.56.edge_ref, f32[4,8192]{1,0:T(4,128)} %cw_ref.5), custom_call_target="tpu_custom_call", output_to_operand_aliasing={{}: (0, {})} | custom-call | tf_op jit(solution)/shard_map/last_rows/pallas_call | solution.py:867
  260.8 0.0 copy-done
  260.8 0.6 slice.30
  261.4 0.6 slice_bitcast_fusion
  262.1 0.1 convert_bitcast_fusion
  262.1 0.2 copy.24
  262.4 0.3 reshape.52
  262.7 0.7 fusion
  263.4 0.7 slice.38
  264.1 0.8 slice.41
  (1 shorter events, 0.0 us)
Async XLA Ops:
  257.9 2.8 %copy-start = (f32[80,512]{1,0:T(8,128)S(1)}, f32[80,512]{1,0:T(8,128)}, u32[]{:S(2)}) copy-start(f32[80,512]{1,0:T(8,128)} %get-tuple-element.58) | copy-start | bytes 491524

commit v4 on v3

--- a/solution.py
+++ b/solution.py
@@ -15,8 +15,8 @@
 LOCAL_GROUP, LOCAL_UNROLL = 4, 16
 SHIPMENTS = ((0, 4), (4, 3), (7, 1))
 CHUNKS = 1
-FWD_GROUP, FWD_UNROLL = 8, 8
-BWD_GROUP, BWD_UNROLL = 8, 8
+FWD_GROUP, FWD_UNROLL = 8, 16
+BWD_GROUP, BWD_UNROLL = 8, 16
 
 
 def logistic(values):
@@ -515,12 +515,11 @@
 
 def reduce_kernel(xpart, dpart, edge, out, all_params, halo, sums, cross, *scratch):
     buffers, plane, scratch = scratch[:48], scratch[48:51], scratch[51:]
-    packed, own_sem, csend, crecv, ssem, rsem, fsend, frecv, psend, precv, qsend, qrecv, hsend, hrecv = scratch
+    own_sem, csend, crecv, ssem, rsem, fsend, frecv, psend, precv, qsend, qrecv, hsend, hrecv = scratch
     d, j, pos, core = place()
     sibling = (pos["y"] * 2 + 1 - core, j)
     following, previous = (d, lax.rem(j + 1, 16)), (d, lax.rem(j + 15, 16))
-    column = [(lax.rem(pos["y"] + k // 2, 4) * 2 + lax.rem(core + k, 2), j) for k in range(1, 8)]
-    greet(planes(pos, core) + column + [following])
+    greet(planes(pos, core) + [sibling, following])
     sent = []
     hops = (2, 1, -1, 0)
     half = 256
@@ -628,20 +627,17 @@
     for p in parts:
         one, two, three = ORDERS[p]
         outer.append([step(p, i, three, {two: spot(two, hops[i])}, [one]) for i in range(4)])
-    for i in range(4):
-        for p in parts:
-            add_core(p, i)
-            outer[p][i][0]()
-    for i in range(4):
+    def relays(p, i):
         for which in (0, 1):
-            for p in parts:
-                outer[p][i][1](which)
-    for i in range(4):
-        for p in parts:
+            outer[p][i][1](which)
+
+    def finish(p):
+        for i in range(4):
             outer[p][i][2]()
             for k in turn[i]:
                 go(direct(p, k))
-    for p in parts:
+
+    def total(p):
         row, count = ROWS[p]
         rows = pl.ds(row, count)
         for k in range(15):
@@ -654,34 +650,53 @@
 
         lax.fori_loop(0, 15, one_more, 0)
 
-    packed[...] = jnp.zeros((16, 128), jnp.bfloat16)
+    def place_of(hops):
+        return all_params.at[lax.rem(pos["z"] + 4 - hops[0], 4), lax.rem(pos["x"] + 4 - hops[1], 4), pos["y"], core]
+
+    def flat(k):
+        return remote(place_of((0, 0)), place_of((0, 0)), psend.at[k], precv.at[k], peer2(pos, core, "zx", OTHERS[k]))
+
+    def upright(hop):
+        ours = all_params.at[:, :, pos["y"], core]
+        return remote(ours, ours, qsend.at[hop], qrecv.at[hop], peer(pos, core, "y", hop))
+
+    for i in range(4):
+        for p in (1, 0, 2):
+            add_core(p, i)
+            outer[p][i][0]()
+    for i in range(2):
+        relays(1, 2 * i)
+        for p in (0, 2):
+            relays(p, i)
+        relays(1, 2 * i + 1)
+    finish(1)
+    for p in (0, 2):
+        relays(p, 2)
+    total(1)
+
     rowsum = jnp.concatenate(
         [out[36 + q:37 + q, 128 * s:128 * s + 128] for q in range(3) for s in range(4)] + [jnp.zeros((4, 128), jnp.float32)], axis=0
     )
-    packed[...] = rowsum.astype(jnp.bfloat16)
-    all_params[pos["z"], pos["x"], pos["y"], core] = packed[...]
-
-    def place_of(hops):
-        return all_params.at[lax.rem(pos["z"] + 4 - hops[0], 4), lax.rem(pos["x"] + 4 - hops[1], 4), pos["y"], core]
-
-    def flat(k):
-        return remote(place_of((0, 0)), place_of((0, 0)), psend.at[k], precv.at[k], peer2(pos, core, "zx", OTHERS[k]))
-
-    def upright(k):
-        ours = all_params.at[:, :, pos["y"], core]
-        return remote(ours, ours, qsend.at[k], qrecv.at[k], column[k - 1])
-
+    all_params[pos["z"], pos["x"], pos["y"], core] = rowsum.astype(jnp.bfloat16)
     for k in range(15):
         go(flat(k))
+    for p in (0, 2):
+        relays(p, 3)
+    for p in (0, 2):
+        finish(p)
     for k in range(15):
         there = place_of(OTHERS[k])
         remote(there, there, psend.at[k], precv.at[k], peer2(pos, core, "zx", OTHERS[k])).wait_recv()
-    for k in range(1, 8):
-        go(upright(k))
-    for k in range(1, 8):
-        y, c = lax.rem(pos["y"] + 4 - k // 2, 4), lax.rem(core + k, 2)
-        there = all_params.at[:, :, y, c]
-        remote(there, there, qsend.at[k], qrecv.at[k], column[k - 1]).wait_recv()
+    for hop in (1, 2, 3):
+        go(upright(hop))
+    total(0)
+    for hop in (1, 2, 3):
+        there = all_params.at[:, :, lax.rem(pos["y"] + 4 - hop, 4), core]
+        remote(there, there, qsend.at[hop], qrecv.at[hop], peer(pos, core, "y", hop)).wait_recv()
+    ours, theirs = all_params.at[:, :, :, core], all_params.at[:, :, :, 1 - core]
+    go(remote(ours, ours, qsend.at[0], qrecv.at[0], sibling))
+    total(2)
+    remote(theirs, theirs, qsend.at[0], qrecv.at[0], sibling).wait_recv()
     edge_copy.wait_recv()
     for copy in sent:
         copy.wait_send()
@@ -707,9 +722,8 @@
         in_specs=[anyspace] * 3,
         out_specs=[vmem, vmem, anyspace],
         scratch_shapes=[pltpu.VMEM((4, 4, 4, 80, 512), bf16)] * 2 + buffers + [
-            pltpu.VMEM((16, 128), bf16),
             dma((3, 4)), dma((3, 4)), dma((3, 4)), dma((3, 4, 4)), dma((3, 4, 4)), dma((3, 15)), dma((3, 15)),
-            dma((15,)), dma((15,)), dma((8,)), dma((8,)), dma, dma,
+            dma((15,)), dma((15,)), dma((4,)), dma((4,)), dma, dma,
         ],
         compiler_params=pltpu.CompilerParams(
             collective_id=2, has_side_effects=True, vmem_limit_bytes=VMEM_LIMIT

time: 266 us -> 254 us (0.955)
  Pallas kernels: 254 us -> 242 us
    pallas_call x1, Pallas kernels: 54.3 us -> 45.7 us  [reduce_all(): pl.pallas_call(reduce_kernel, name='reduce_shards', out_shape=[jax.ShapeD...]
    pallas_call x1, Pallas kernels: 79.4 us -> 76.5 us  [main_scan(): pl.pallas_call(main_scan_kernel, grid=(C,), name='main_scan', in_specs=[t...]
where the time goes in v4:
time: 254 us; the launch traced here: 253 us
  Pallas kernels  242 us (95%)
  local copies, waits for them, and re-layouts  6.81 us (3%)
  other arithmetic  3.65 us (1%)
    pallas_call x1, Pallas kernels, main_scan(): pl.pallas_call(main_scan_kernel, grid=(C,), name='main_scan', in_specs=[t...  76.5 us
    pallas_call x1, Pallas kernels, local_scan(): pl.pallas_call(local_scan_kernel, grid=(C,), name='local_scan', in_specs=...  45.7 us
    pallas_call x1, Pallas kernels, reduce_all(): pl.pallas_call(reduce_kernel, name='reduce_shards', out_shape=[jax.ShapeD...  45.7 us
    pallas_call x1, Pallas kernels, gather(): pl.pallas_call(functools.partial(gather_kernel, parts, tail is not None),...  43.6 us
    pallas_call x1, Pallas kernels, weight_grads(): pl.pallas_call(grads_kernel, grid=(E // 1024,), name='weight_grads', in_s...  16.4 us
    pallas_call x1, Pallas kernels, conv_project(): pl.pallas_call(conv_kernel, grid=(E // 1024,), name='conv_project', in_sp...  11.5 us

profile of v4, /device:TPU:1, one launch (start us, length us, event | category | flops | bytes accessed | tf_op | source)
XLA Modules:
  0.0 253.4 jit_solution(13308934997868531657)
XLA Ops:
  0.7 0.1 pad.1.clone
  0.7 1.5 pad_maximum_fusion.refs_0_
  2.2 0.9 convert_bitcast_fusion.1
  3.2 0.6 copy.29
  3.8 1.1 multiply_bitcast_fusion
  4.9 0.9 copy.27
  5.8 43.6 %gather_shards.1 = (bf16[4,4,4,2,80,512]{5,4,3,2,1,0:T(8,128)(2,1)}, f32[3,64,128]{2,1,0:T(8,128)}) custom-call(bf16[80,512]{1,0:T(8,128)(2,1)} %pad_maximum_fusion.refs_0_, f32[3,64,128]{2,1,0:T(8,128)} %bitcast.53), custom_call_target="tpu_custom_call" | custom-call | tf_op jit(solution)/shard_map/gather_shards/pallas_call | solution.py:505
  49.5 11.5 %conv_project.1 = (bf16[128,8192]{1,0:T(8,128)(2,1)}, bf16[128,256]{1,0:T(8,128)(2,1)}, f32[32,128,128]{2,1,0:T(8,128)}) custom-call(bf16[128,8192]{1,0:T(8,128)(2,1)} %bitcast.39, f32[3,64,128]{2,1,0:T(8,128)} %get-tuple-element.35.halo_ref, f32[4,8192]{1,0:T(4,128)} %cw_ref.5, f32[1,8192]{1,0:T(1,128)} %bitcast.54, bf16[16,8,80,512]{3,2,1,0:T(8,128)(2,1)} %bitcast.33), custom_call_target="tpu_custom_call" | custom-call | tf_op jit(solution)/shard_map/conv_project/pallas_call | solution.py:794
  60.9 45.7 %local_scan.1 = (f32[128,64,128]{2,1,0:T(8,128)}, f32[128,64,128]{2,1,0:T(8,128)}, f32[128,64,128]{2,1,0:T(8,128)}, f32[128,8192]{1,0:T(8,128)}, bf16[16,8,16,128]{3,2,1,0:T(8,128)(2,1)}) custom-call(bf16[128,256]{1,0:T(8,128)(2,1)} %get-tuple-element.37.low_ref, bf16[16,8,80,512]{3,2,1,0:T(8,128)(2,1)} %bitcast.34, bf16[16,8,80,512]{3,2,1,0:T(8,128)(2,1)} %bitcast.35, ...), custom_call_target="tpu_custom_call" | custom-call | tf_op jit(solution)/shard_map/local_scan/pallas_call | solution.py:160
  106.6 76.5 %main_scan.1 = (bf16[128,8192]{1,0:T(8,128)(2,1)}, bf16[128,8192]{1,0:T(8,128)(2,1)}, f32[128,8192]{1,0:T(8,128)}, bf16[16,8,32,512]{3,2,1,0:T(8,128)(2,1)}, f32...) custom-call(f32[128,64,128]{2,1,0:T(8,128)} %get-tuple-element.40.step_ref, ...), custom_call_target="tpu_custom_call" | custom-call | tf_op jit(solution)/shard_map/main_scan/pallas_call | solution.py:312
  183.1 16.4 %weight_grads.1 = (bf16[128,8192]{1,0:T(8,128)(2,1)}, f32[3,64,128]{2,1,0:T(8,128)}, f32[16,8192]{1,0:T(8,128)}, bf16[16,8,48,512]{3,2,1,0:T(8,128)(2,1)}) custom-call(f32[128,256]{1,0:T(8,128)} %get-tuple-element.46.glow_ref, f32[128,32]{1,0:T(8,128)} %get-tuple-element.47.gbc_ref, f32[128,8192]{1,0:T(8,128)} %get-tuple-element.48.gcx_ref, ...), custom_call_target="tpu_custom_call" | custom-call | tf_op jit(solution)/shard_map/weight_grads/pallas_call | solution.py:852
  199.6 45.7 %reduce_shards.1 = (f32[80,512]{1,0:T(8,128)}, bf16[4,4,4,2,16,128]{5,4,3,2,1,0:T(8,128)(2,1)}, f32[3,64,128]{2,1,0:T(8,128)}) custom-call(bf16[4,4,4,2,48,512]{5,4,3,2,1,0:T(8,128)(2,1)} %bitcast.48, bf16[4,4,4,2,32,512]{5,4,3,2,1,0:T(8,128)(2,1)} %bitcast.49, f32[3,64,128]{2,1,0:T(8,128)} %get-tuple-element.55.edge), custom_call_target="tpu_custom_call" | custom-call | tf_op jit(solution)/shard_map/reduce_shards/pallas_call | solution.py:714
  245.2 1.1 copy.25
  246.4 0.0 copy-start
  246.4 2.8 %last_rows.1 = bf16[128,8192]{1,0:T(8,128)(2,1)} custom-call(bf16[128,8192]{1,0:T(8,128)(2,1)} %get-tuple-element.51.gx_ref, f32[16,8192]{1,0:T(8,128)} %get-tuple-element.52.tail_ref, f32[3,64,128]{2,1,0:T(8,128)} %get-tuple-element.56.edge_ref, f32[4,8192]{1,0:T(4,128)} %cw_ref.5), custom_call_target="tpu_custom_call", output_to_operand_aliasing={{}: (0, {})} | custom-call | tf_op jit(solution)/shard_map/last_rows/pallas_call | solution.py:881
  249.2 0.0 copy-done
  249.2 0.6 slice.30
  249.9 0.6 slice_bitcast_fusion
  250.5 0.1 convert_bitcast_fusion
  250.6 0.2 copy.24
  250.8 0.3 reshape.52
  251.2 0.7 fusion
  251.9 0.7 slice.38
  252.5 0.8 slice.41
  (1 shorter events, 0.0 us)
Async XLA Ops:
  246.4 2.8 %copy-start = (f32[80,512]{1,0:T(8,128)S(1)}, f32[80,512]{1,0:T(8,128)}, u32[]{:S(2)}) copy-start(f32[80,512]{1,0:T(8,128)} %get-tuple-element.58) | copy-start | bytes 491524

commit v5 on v4

--- a/solution.py
+++ b/solution.py
@@ -15,8 +15,8 @@
 LOCAL_GROUP, LOCAL_UNROLL = 4, 16
 SHIPMENTS = ((0, 4), (4, 3), (7, 1))
 CHUNKS = 1
-FWD_GROUP, FWD_UNROLL = 8, 16
-BWD_GROUP, BWD_UNROLL = 8, 16
+FWD_GROUP, FWD_UNROLL = 16, 16
+BWD_GROUP, BWD_UNROLL = 16, 16
 
 
 def logistic(values):

time: 254 us -> 253 us (level)
  no operation moved by 1% of the time
where the time goes in v5:
time: 253 us
  Pallas kernels  242 us (96%)
  local copies, waits for them, and re-layouts  6.81 us (3%)
  other arithmetic  3.65 us (1%)
    pallas_call x1, Pallas kernels, main_scan(): pl.pallas_call(main_scan_kernel, grid=(C,), name='main_scan', in_specs=[t...  75.9 us
    pallas_call x1, Pallas kernels, local_scan(): pl.pallas_call(local_scan_kernel, grid=(C,), name='local_scan', in_specs=...  45.7 us
    pallas_call x1, Pallas kernels, reduce_all(): pl.pallas_call(reduce_kernel, name='reduce_shards', out_shape=[jax.ShapeD...  45.7 us
    pallas_call x1, Pallas kernels, gather(): pl.pallas_call(functools.partial(gather_kernel, parts, tail is not None),...  43.6 us
    pallas_call x1, Pallas kernels, weight_grads(): pl.pallas_call(grads_kernel, grid=(E // 1024,), name='weight_grads', in_s...  16.4 us
    pallas_call x1, Pallas kernels, conv_project(): pl.pallas_call(conv_kernel, grid=(E // 1024,), name='conv_project', in_sp...  11.5 us

profile of v5, /device:TPU:1, one launch (start us, length us, event | category | flops | bytes accessed | tf_op | source)
XLA Modules:
  0.0 252.7 jit_solution(6710126556813864627)
XLA Ops:
  0.7 0.1 pad.1.clone
  0.7 1.5 pad_maximum_fusion.refs_0_
  2.2 0.9 convert_bitcast_fusion.1
  3.2 0.6 copy.29
  3.8 1.1 multiply_bitcast_fusion
  4.9 0.9 copy.27
  5.8 43.6 %gather_shards.1 = (bf16[4,4,4,2,80,512]{5,4,3,2,1,0:T(8,128)(2,1)}, f32[3,64,128]{2,1,0:T(8,128)}) custom-call(bf16[80,512]{1,0:T(8,128)(2,1)} %pad_maximum_fusion.refs_0_, f32[3,64,128]{2,1,0:T(8,128)} %bitcast.53), custom_call_target="tpu_custom_call" | custom-call | tf_op jit(solution)/shard_map/gather_shards/pallas_call | solution.py:505
  49.5 11.5 %conv_project.1 = (bf16[128,8192]{1,0:T(8,128)(2,1)}, bf16[128,256]{1,0:T(8,128)(2,1)}, f32[32,128,128]{2,1,0:T(8,128)}) custom-call(bf16[128,8192]{1,0:T(8,128)(2,1)} %bitcast.39, f32[3,64,128]{2,1,0:T(8,128)} %get-tuple-element.35.halo_ref, f32[4,8192]{1,0:T(4,128)} %cw_ref.5, f32[1,8192]{1,0:T(1,128)} %bitcast.54, bf16[16,8,80,512]{3,2,1,0:T(8,128)(2,1)} %bitcast.33), custom_call_target="tpu_custom_call" | custom-call | tf_op jit(solution)/shard_map/conv_project/pallas_call | solution.py:794
  60.9 45.7 %local_scan.1 = (f32[128,64,128]{2,1,0:T(8,128)}, f32[128,64,128]{2,1,0:T(8,128)}, f32[128,64,128]{2,1,0:T(8,128)}, f32[128,8192]{1,0:T(8,128)}, bf16[16,8,16,128]{3,2,1,0:T(8,128)(2,1)}) custom-call(bf16[128,256]{1,0:T(8,128)(2,1)} %get-tuple-element.37.low_ref, bf16[16,8,80,512]{3,2,1,0:T(8,128)(2,1)} %bitcast.34, bf16[16,8,80,512]{3,2,1,0:T(8,128)(2,1)} %bitcast.35, ...), custom_call_target="tpu_custom_call" | custom-call | tf_op jit(solution)/shard_map/local_scan/pallas_call | solution.py:160
  106.6 75.9 %main_scan.1 = (bf16[128,8192]{1,0:T(8,128)(2,1)}, bf16[128,8192]{1,0:T(8,128)(2,1)}, f32[128,8192]{1,0:T(8,128)}, bf16[16,8,32,512]{3,2,1,0:T(8,128)(2,1)}, f32...) custom-call(f32[128,64,128]{2,1,0:T(8,128)} %get-tuple-element.40.step_ref, ...), custom_call_target="tpu_custom_call" | custom-call | tf_op jit(solution)/shard_map/main_scan/pallas_call | solution.py:312
  182.5 16.4 %weight_grads.1 = (bf16[128,8192]{1,0:T(8,128)(2,1)}, f32[3,64,128]{2,1,0:T(8,128)}, f32[16,8192]{1,0:T(8,128)}, bf16[16,8,48,512]{3,2,1,0:T(8,128)(2,1)}) custom-call(f32[128,256]{1,0:T(8,128)} %get-tuple-element.46.glow_ref, f32[128,32]{1,0:T(8,128)} %get-tuple-element.47.gbc_ref, f32[128,8192]{1,0:T(8,128)} %get-tuple-element.48.gcx_ref, ...), custom_call_target="tpu_custom_call" | custom-call | tf_op jit(solution)/shard_map/weight_grads/pallas_call | solution.py:852
  198.9 45.7 %reduce_shards.1 = (f32[80,512]{1,0:T(8,128)}, bf16[4,4,4,2,16,128]{5,4,3,2,1,0:T(8,128)(2,1)}, f32[3,64,128]{2,1,0:T(8,128)}) custom-call(bf16[4,4,4,2,48,512]{5,4,3,2,1,0:T(8,128)(2,1)} %bitcast.48, bf16[4,4,4,2,32,512]{5,4,3,2,1,0:T(8,128)(2,1)} %bitcast.49, f32[3,64,128]{2,1,0:T(8,128)} %get-tuple-element.55.edge), custom_call_target="tpu_custom_call" | custom-call | tf_op jit(solution)/shard_map/reduce_shards/pallas_call | solution.py:714
  244.6 1.1 copy.25
  245.8 0.0 copy-start
  245.8 2.8 %last_rows.1 = bf16[128,8192]{1,0:T(8,128)(2,1)} custom-call(bf16[128,8192]{1,0:T(8,128)(2,1)} %get-tuple-element.51.gx_ref, f32[16,8192]{1,0:T(8,128)} %get-tuple-element.52.tail_ref, f32[3,64,128]{2,1,0:T(8,128)} %get-tuple-element.56.edge_ref, f32[4,8192]{1,0:T(4,128)} %cw_ref.5), custom_call_target="tpu_custom_call", output_to_operand_aliasing={{}: (0, {})} | custom-call | tf_op jit(solution)/shard_map/last_rows/pallas_call | solution.py:881
  248.6 0.0 copy-done
  248.6 0.6 slice.30
  249.2 0.6 slice_bitcast_fusion
  249.9 0.1 convert_bitcast_fusion
  250.0 0.2 copy.24
  250.2 0.3 reshape.52
  250.5 0.7 fusion
  251.2 0.7 slice.38
  251.9 0.8 slice.41
  (1 shorter events, 0.0 us)
Async XLA Ops:
  245.8 2.8 %copy-start = (f32[80,512]{1,0:T(8,128)S(1)}, f32[80,512]{1,0:T(8,128)}, u32[]{:S(2)}) copy-start(f32[80,512]{1,0:T(8,128)} %get-tuple-element.58) | copy-start | bytes 491524
